TPU v7x, 256 devices: a whole 4x4x8 slice. The times are simulated.
256 devices in a mesh: dp: 64 (over y_hi, z, x), factor: 4 (over y_lo, core).
Axes of the slice: x: 4, y: 4 (y_hi: 2, y_lo: 2; y = y_hi * 2 + y_lo), z: 8, core: 2. Of those that a mesh axis runs over, the one named last changes fastest.
Arguments:
- acts: bfloat16 [49152, 4096], P('dp', 'factor'), may hold values from -400 to 400
Outputs:
- act_factor: float32 [2, 4096, 1024], P(None, ('factor', 'dp'))
All inputs are finite; a program needn't handle non-finite values.
Results may differ from a plain program's by a relative error of at most 0.0003.
Values may be sent and summed in bfloat16 or wider, within the bound.
No kernel may reach another device: no remote copies, remote signals or barrier semaphores. Data moves between devices by JAX's collectives and lax.ppermute only.
A program may use at most 64 MiB of HBM per device.

v0:
```python
import jax
import jax.numpy as jnp
from jax import lax
from jax.sharding import PartitionSpec as P


def passed_along(value, axis, by):
    length = lax.axis_size(axis)
    return lax.ppermute(value, axis, [(i, (i + by) % length) for i in range(length)])


def block_rows(own, partner, scale):
    product = jnp.einsum("tc,tj->cj", own, partner, preferred_element_type=jnp.float32)
    return product * scale


def per_device(acts):
    scale = 1.0 / (acts.shape[0] * lax.axis_size("dp"))
    partners = [acts]
    current = acts
    current = passed_along(current, "factor", -1)
    partners.append(current)
    whole = jnp.stack([block_rows(acts, partner, scale) for partner in partners], axis=0)
    summed = lax.psum_scatter(whole, "dp", scatter_dimension=1, tiled=True)
    return summed


def solution(mesh):
    return jax.shard_map(
        per_device,
        mesh=mesh,
        in_specs=(P("dp", "factor"),),
        out_specs=P(None, ("factor", "dp"), None),
        check_vma=False,
    )
```

profile of v0, /device:TPU:8, one launch (start us, length us, event | category | flops | bytes accessed | tf_op | source)
XLA Modules:
  0.0 421.1 jit_solution(17648361737659609621)
XLA Ops:
  6.5 0.0 copy-start
  6.5 0.0 reduce-scatter.2.cloned.1.call-start
  6.5 0.0 collective-permute-start
  6.5 3.9 multiply_bitcast_fusion.1
  10.5 14.4 %collective-permute-done = bf16[768,1024]{1,0:T(8,128)(2,1)S(1)} collective-permute-done((bf16[768,1024]{1,0:T(8,128)(2,1)}, bf16[768,1024]{1,0:T(8,128)(2,1)S(1)}, u32[]{:S(2)}, u32[]{:S(2)}) %collective-permute-start) | collective-permute-done | bytes 1572896 | tf_op jit(solution)/shard_map/ppermute | solution.py:9
  24.9 0.0 copy-done
  24.9 1.9 multiply_bitcast_fusion
  26.7 4.1 pad_maximum_fusion
  30.8 0.0 reduce-scatter.2.cloned.1.call-update
  30.8 383.4 %reduce-scatter.2.cloned.1.call-done = f32[2,16,1024]{2,1,0:T(8,128)} async-done(((f32[2,1024,1024]{2,1,0:T(8,128)}), f32[2,16,1024]{2,1,0:T(8,128)}) %reduce-scatter.2.cloned.1.call-update) | async-done | bytes 131088 | tf_op jit(solution)/shard_map/reduce_scatter | solution.py:24
Async XLA Ops:
  6.5 18.3 %copy-start = (bf16[768,1024]{1,0:T(8,128)(2,1)S(1)}, bf16[768,1024]{1,0:T(8,128)(2,1)}, u32[]{:S(2)}) copy-start(bf16[768,1024]{1,0:T(8,128)(2,1)} %param.1) | copy-start | bytes 4718596
  6.5 407.7 %reduce-scatter.2.cloned.1.call-start = ((), (), s32[]{:S(2)}) async-start(), calls=%async_computation.1 | async-start | bytes 8519680 | tf_op jit(solution)/shard_map/reduce_scatter | solution.py:24
  6.5 18.3 %collective-permute-start = (bf16[768,1024]{1,0:T(8,128)(2,1)}, bf16[768,1024]{1,0:T(8,128)(2,1)S(1)}, u32[]{:S(2)}, u32[]{:S(2)}) collective-permute-start(bf16[768,1024]{1,0:T(8,128)(2,1)} %param.1), channel_id=1, source_target_pairs={{0,3},{1,0},{2,1},{3,2},{4,7},{5,4},{6,5},{7,6},{8,11},{9,8},{10,9... | collective-permute-start | bytes 4718600 | tf_op jit(solution)/shard_map/ppermute | solution.py:9
Sparse Core Ops, SparseCore 0:
  31.0 383.2 reduce-scatter.1
where the time goes:
time: 421 us
  waiting for transfers between devices  398 us (95%)
  between operations  13.4 us (3%)
  matrix products  5.79 us (1%)
    reduce_scatter x1, waiting for transfers between devices, per_device(): summed = lax.psum_scatter(whole, 'dp', scatter_dimension=1, tiled=True)  383 us
    ppermute x1, waiting for transfers between devices, passed_along(): lax.ppermute(value, axis, [(i, (i + by) % length) for i in range(length)])  14.4 us
  transfers between devices with their start and end apart: 2, of which 2 were waited for; matrix products, arithmetic and copies ran while one was open for 1% of the time, Pallas kernels for 0%

commit v1 on v0

v1 whole, which is shorter than its diff:
```python
import functools

import jax
import jax.numpy as jnp
from jax import lax
from jax.experimental import pallas as pl
from jax.experimental.pallas import tpu as pltpu
from jax.sharding import Mesh, PartitionSpec as P

SIZES = {"yh": 2, "z": 8, "x": 4, "yl": 2, "core": 2}
DP = ("yh", "z", "x")
FACTOR = ("yl", "core")
YZ = ("yh", "z")
NX, NYZ = SIZES["x"], SIZES["yh"] * SIZES["z"]
NF = SIZES["yl"] * SIZES["core"]
TOP = 15.0
VMEM = 48 * 1024 * 1024


def share(index, count):
    return 1.0 - 0.5 * jnp.float32(index) / count


def lifted(power, factor):
    return jnp.max(jnp.exp2(jnp.full((8, 128), TOP - power))) * factor


def lowered(power, factor):
    return jnp.max(jnp.exp2(jnp.full((8, 128), power - TOP))) / factor


def gram_kernel(own_ref, partner_ref, out_ref):
    tokens, panel = own_ref.shape
    count = panel // NX
    rows = panel // (NX * NYZ)
    here = lax.axis_index("x")
    largest = lambda ref: jnp.max(jnp.abs(ref[...]).astype(jnp.float32))
    bound = tokens * (largest(own_ref) + 1e-15) * (largest(partner_ref) + 1e-15)
    power = jnp.max(jnp.ceil(jnp.log2(jnp.full((8, 128), bound))))
    up = lifted(power, share(here, NX))
    for by in range(NX):
        out_ref[by, count:, :] = jnp.full((8, panel), power)
    chunk = 256
    for c in range(panel // chunk):
        product = lax.dot_general(
            own_ref[:, c * chunk : (c + 1) * chunk], partner_ref[...], (((0,), (0,)), ((), ())),
            preferred_element_type=jnp.float32,
        ) * up
        for n in range(chunk // rows):
            yz, x = divmod(c * (chunk // rows) + n, NX)
            by = lax.rem(x - here + NX, NX)
            out_ref[by, yz * rows : (yz + 1) * rows, :] = product[n * rows : (n + 1) * rows]


def gram(own, partner):
    tokens, panel = own.shape
    return pl.pallas_call(
        gram_kernel,
        out_shape=jax.ShapeDtypeStruct((NX, panel // NX + 8, panel), jnp.float32),
        in_specs=[pl.BlockSpec(memory_space=pltpu.VMEM)] * 2,
        out_specs=pl.BlockSpec(memory_space=pltpu.VMEM),
        compiler_params=pltpu.CompilerParams(vmem_limit_bytes=VMEM),
        cost_estimate=pl.CostEstimate(flops=2 * tokens * panel * panel, bytes_accessed=8 << 20, transcendentals=0),
        name="gram",
    )(own, partner)


def x_sum_kernel(own_ref, *refs):
    others, out_ref = refs[:-1], refs[-1]
    count, panel = own_ref.shape[1] - 8, own_ref.shape[2]
    here = lax.axis_index("x")
    power_of = lambda block: jnp.max(block[count:, :128])
    blocks = [own_ref.at[0], *others]
    powers = [power_of(block) for block in blocks]
    power = functools.reduce(jnp.maximum, powers) + 2.0
    iyz = lax.axis_index("yh") * SIZES["z"] + lax.axis_index("z")
    up = lifted(power, share(iyz, NYZ))
    weights = [lowered(p, share(lax.rem(here - by + NX, NX), NX)) * up for by, p in enumerate(powers)]
    rows = count // NYZ
    for n in range(NYZ):
        part = pl.ds(n * rows, rows)
        out_ref[n, :, :panel] = functools.reduce(
            lambda a, b: a + b, [block[part, :] * w for block, w in zip(blocks, weights)]
        )
        out_ref[n, :, panel:] = jnp.full((rows, 128), power)


def x_sum(own, others):
    _, count, panel = own.shape
    rows = (count - 8) // NYZ
    return pl.pallas_call(
        x_sum_kernel,
        grid=(1,),
        out_shape=jax.ShapeDtypeStruct((NYZ, rows, panel + 128), jnp.float32),
        in_specs=[pl.BlockSpec((1, count, panel), lambda i: (0, 0, 0))]
        + [pl.BlockSpec((count, panel), lambda i: (0, 0))] * (NX - 1),
        out_specs=pl.BlockSpec((NYZ, rows, panel + 128), lambda i: (0, 0, 0)),
        compiler_params=pltpu.CompilerParams(vmem_limit_bytes=VMEM),
        cost_estimate=pl.CostEstimate(flops=8 << 18, bytes_accessed=5 << 20, transcendentals=0),
        name="x_sum",
    )(own, *others)


def yz_sum_kernel(scale, got_ref, out_ref):
    panel = out_ref.shape[2]
    for k in range(2):
        weights = [
            jnp.exp2(got_ref[s, k, :, panel:] - TOP) * (scale / float(1.0 - 0.5 * s / NYZ)) for s in range(NYZ)
        ]
        for j in range(panel // 128):
            part = slice(j * 128, (j + 1) * 128)
            out_ref[k, :, part] = functools.reduce(
                lambda a, b: a + b, [got_ref[s, k, :, part] * w for s, w in enumerate(weights)]
            )


def yz_sum(got, scale):
    _, _, rows, wide = got.shape
    return pl.pallas_call(
        functools.partial(yz_sum_kernel, scale),
        out_shape=jax.ShapeDtypeStruct((2, rows, wide - 128), jnp.float32),
        in_specs=[pl.BlockSpec(memory_space=pltpu.VMEM)],
        out_specs=pl.BlockSpec(memory_space=pltpu.VMEM),
        compiler_params=pltpu.CompilerParams(vmem_limit_bytes=VMEM),
        cost_estimate=pl.CostEstimate(flops=1 << 20, bytes_accessed=3 << 20, transcendentals=0),
        name="yz_sum",
    )(got)


def per_device(acts):
    tokens, panel = acts.shape
    scale = 1.0 / (tokens * NX * NYZ)
    partner = lax.ppermute(acts, FACTOR, [(i, (i - 1) % NF) for i in range(NF)])

    def over_x(other):
        scaled = gram(acts, other)
        got = [None] * (NX - 1)
        for by in (2, 1, 3):
            pairs = [(i, (i + by) % NX) for i in range(NX)]
            got[by - 1] = lax.ppermute(scaled[by].astype(jnp.float16), "x", pairs).astype(jnp.float32)
        return x_sum(scaled, got)

    both = jnp.stack([over_x(acts), over_x(partner)], axis=1).astype(jnp.float16)
    got = lax.all_to_all(both, YZ, 0, 0, tiled=True)
    return yz_sum(got.astype(jnp.float32), scale)


def solution(mesh):
    fine = Mesh(mesh.devices.reshape(tuple(SIZES.values())), tuple(SIZES))
    return jax.shard_map(
        per_device,
        mesh=fine,
        in_specs=(P(DP, FACTOR),),
        out_specs=P(None, FACTOR + DP, None),
        check_vma=False,
    )
```

time: 421 us -> 106 us (0.25)
  waiting for transfers between devices: 398 us -> 35.8 us
  blocking collectives: 0 us -> 42.8 us
  between operations: 13.4 us -> 0.16 us
  Pallas kernels: 0 us -> 10.7 us
  starting transfers between devices: 0.01 us -> 8.19 us
  matrix products: 5.79 us -> 0 us
    reduce_scatter x1 -> x0, waiting for transfers between devices: 383 us -> none  [per_device(): summed = lax.psum_scatter(whole, 'dp', scatter_dimension=1, tiled=True)]
    all_to_all x0 -> x1, blocking collectives: none -> 42.8 us  [per_device(): got = lax.all_to_all(both, YZ, 0, 0, tiled=True)]
    ppermute x1 -> x7, waiting for transfers between devices: 14.4 us -> 35.8 us  [the longest x6 28.2 us: over_x(): lax.ppermute(scaled[by].astype(jnp.float16), 'x', pairs).astype(jnp.float32)]
    pallas_call x0 -> x5, Pallas kernels: none -> 10.7 us  [the longest x2 6.44 us: gram(): pl.pallas_call(gram_kernel, out_shape=jax.ShapeDtypeStruct((NX, panel //...]
    ppermute x1 -> x7, starting transfers between devices: 0.01 us -> 8.19 us  [the longest x6 8.19 us: over_x(): lax.ppermute(scaled[by].astype(jnp.float16), 'x', pairs).astype(jnp.float32)]
    dot_general x2 -> x0, matrix products: 5.79 us -> none  [block_rows(): jnp.einsum('tc,tj->cj', own, partner, preferred_element_type=jnp.float32)]
  transfers between devices with their start and end apart: 2 -> 7, of which waited for: 2 -> 5; matrix products, arithmetic and copies ran while one was open for 1% -> 4% of each run, Pallas kernels for 0% -> 8%
where the time goes in v1:
time: 106 us
  blocking collectives  42.8 us (40%)
  waiting for transfers between devices  35.8 us (34%)
  Pallas kernels  10.7 us (10%)
  starting transfers between devices  8.19 us (8%)
  other arithmetic  4.17 us (4%)
  local copies, waits for them, and re-layouts  3.95 us (4%)
    all_to_all x1, blocking collectives, per_device(): got = lax.all_to_all(both, YZ, 0, 0, tiled=True)  42.8 us
    ppermute x6, waiting for transfers between devices, over_x(): lax.ppermute(scaled[by].astype(jnp.float16), 'x', pairs).astype(jnp.float32)  28.2 us
    ppermute x6, starting transfers between devices, over_x(): lax.ppermute(scaled[by].astype(jnp.float16), 'x', pairs).astype(jnp.float32)  8.19 us
    ppermute x1, waiting for transfers between devices, per_device(): partner = lax.ppermute(acts, FACTOR, [(i, (i - 1) % NF) for i in range(NF)])  7.55 us
    pallas_call x2, Pallas kernels, gram(): pl.pallas_call(gram_kernel, out_shape=jax.ShapeDtypeStruct((NX, panel //...  6.44 us
    pallas_call x2, Pallas kernels, x_sum(): pl.pallas_call(x_sum_kernel, grid=(1,), out_shape=jax.ShapeDtypeStruct((N...  3.41 us
    another operation x2, other arithmetic  3.07 us
    unnamed x4, local copies, waits for them, and re-layouts  3.05 us
  transfers between devices with their start and end apart: 7, of which 5 were waited for; matrix products, arithmetic and copies ran while one was open for 4% of the time, Pallas kernels for 8%

profile of v1, /device:TPU:8, one launch (start us, length us, event | category | flops | bytes accessed | tf_op | source)
XLA Modules:
  0.0 105.8 jit_solution(5852459120061127947)
XLA Ops:
  0.0 1.4 %copy-done.1 = bf16[768,1024]{1,0:T(8,128)(2,1)S(1)} copy-done((bf16[768,1024]{1,0:T(8,128)(2,1)S(1)}, bf16[768,1024]{1,0:T(8,128)(2,1)}, u32[]{:S(2)}) %copy-start.1) | copy-done | bytes 1572888
  1.4 2.2 %gram.2.own_ref = f32[4,264,1024]{2,1,0:T(8,128)S(1)} custom-call(bf16[768,1024]{1,0:T(8,128)(2,1)S(1)} %copy-done.1, bf16[768,1024]{1,0:T(8,128)(2,1)S(1)} %copy-done.1), custom_call_target="tpu_custom_call" | custom-call | flops 1610612736 | bytes 8388608 | tf_op jit(solution)/shard_map/gram/pallas_call | solution.py:57
  3.7 0.4 convert.18
  4.1 1.6 %copy-done = f32[4,264,1024]{2,1,0:T(8,128)} copy-done((f32[4,264,1024]{2,1,0:T(8,128)}, f32[4,264,1024]{2,1,0:T(8,128)S(1)}, u32[]{:S(2)}) %copy-start) | copy-done | bytes 4325400
  5.7 0.4 slice_bitcast_fusion.3
  6.2 2.8 %collective-permute-start.2 = (f16[264,1024]{1,0:T(8,128)(2,1)S(1)}, f16[264,1024]{1,0:T(8,128)(2,1)S(1)}, u32[]{:S(2)}, u32[]{:S(2)}) collective-permute-start(f16[264,1024]{1,0:T(8,128)(2,1)S(1)} %get-tuple-element.5), channel_id=1, source_target_pairs={{0,12},{4,0},{8,4},{12,8},{1,13},{5,1},{9,5},{13,9},{2,14},{6,2},{... | collective-permute-start | bytes 1622024 | tf_op jit(solution)/shard_map/ppermute | solution.py:140
  9.0 0.8 collective-permute-start.1
  9.8 0.9 collective-permute-start
  10.7 7.5 %collective-permute-done.3.partner_ref = bf16[768,1024]{1,0:T(8,128)(2,1)S(1)} collective-permute-done((bf16[768,1024]{1,0:T(8,128)(2,1)}, bf16[768,1024]{1,0:T(8,128)(2,1)S(1)}, u32[]{:S(2)}, u32[]{:S(2)}) %collective-permute-start.3) | collective-permute-done | bytes 1572896 | tf_op jit(solution)/shard_map/ppermute | solution.py:133
  18.3 4.2 %gram.3.own_ref = f32[4,264,1024]{2,1,0:T(8,128)} custom-call(bf16[768,1024]{1,0:T(8,128)(2,1)S(1)} %copy-done.1, bf16[768,1024]{1,0:T(8,128)(2,1)S(1)} %collective-permute-done.3.partner_ref), custom_call_target="tpu_custom_call" | custom-call | flops 1610612736 | bytes 8388608 | tf_op jit(solution)/shard_map/gram/pallas_call | solution.py:57
  22.5 2.6 %convert.20 = f16[4,264,1024]{2,1,0:T(8,128)(2,1)S(1)} convert(f32[4,264,1024]{2,1,0:T(8,128)} %gram.3.own_ref) | non-fusion elementwise | flops 1081344 | bytes 6488064 | tf_op jit(solution)/shard_map/convert.6
  25.1 0.4 slice_bitcast_fusion
  25.6 2.9 %collective-permute-start.6 = (f16[264,1024]{1,0:T(8,128)(2,1)S(1)}, f16[264,1024]{1,0:T(8,128)(2,1)S(1)}, u32[]{:S(2)}, u32[]{:S(2)}) collective-permute-start(f16[264,1024]{1,0:T(8,128)(2,1)S(1)} %get-tuple-element.8), channel_id=1, source_target_pairs={{0,12},{4,0},{8,4},{12,8},{1,13},{5,1},{9,5},{13,9},{2,14},{6,2},{... | collective-permute-start | bytes 1622024 | tf_op jit(solution)/shard_map/ppermute | solution.py:140
  28.5 0.8 collective-permute-start.5
  29.3 3.8 %collective-permute-done.2 = f16[264,1024]{1,0:T(8,128)(2,1)S(1)} collective-permute-done((f16[264,1024]{1,0:T(8,128)(2,1)S(1)}, f16[264,1024]{1,0:T(8,128)(2,1)S(1)}, u32[]{:S(2)}, u32[]{:S(2)}) %collective-permute-start.2) | collective-permute-done | bytes 540704 | tf_op jit(solution)/shard_map/ppermute | solution.py:140
  33.1 0.1 convert_element_type.51.refs_2_
  33.1 0.0 collective-permute-done.1
  33.2 0.1 convert_element_type.49.refs_1_
  33.2 4.0 %collective-permute-done = f16[264,1024]{1,0:T(8,128)(2,1)S(1)} collective-permute-done((f16[264,1024]{1,0:T(8,128)(2,1)S(1)}, f16[264,1024]{1,0:T(8,128)(2,1)S(1)}, u32[]{:S(2)}, u32[]{:S(2)}) %collective-permute-start) | collective-permute-done | bytes 540704 | tf_op jit(solution)/shard_map/ppermute | solution.py:140
  37.2 0.1 convert_element_type.47.refs_0_
  37.3 1.7 %x_sum.2 = f32[16,16,1152]{2,1,0:T(8,128)S(1)} custom-call(f32[4,264,1024]{2,1,0:T(8,128)} %copy-done, f32[264,1024]{1,0:T(8,128)S(1)} %convert_element_type.47.refs_0_, f32[264,1024]{1,0:T(8,128)S(1)} %convert_element_type.49.refs_1_, f32[264,1024]{1,0:T(8,128)S(1)} %convert_element_type.51.refs_2_), custom_call_target="tpu_custom_call" | custom-call | flops 2097152 | bytes 5242880 | tf_op jit(solution)/shard_map/x_sum/pallas_call | solution.py:91
  39.0 17.0 %collective-permute-done.6 = f16[264,1024]{1,0:T(8,128)(2,1)S(1)} collective-permute-done((f16[264,1024]{1,0:T(8,128)(2,1)S(1)}, f16[264,1024]{1,0:T(8,128)(2,1)S(1)}, u32[]{:S(2)}, u32[]{:S(2)}) %collective-permute-start.6) | collective-permute-done | bytes 540704 | tf_op jit(solution)/shard_map/ppermute | solution.py:140
  56.0 0.1 convert_element_type.57.refs_2_
  56.1 0.1 convert_element_type.55.refs_1_
  56.2 3.5 %collective-permute-done.4 = f16[264,1024]{1,0:T(8,128)(2,1)S(1)} collective-permute-done((f16[264,1024]{1,0:T(8,128)(2,1)S(1)}, f16[264,1024]{1,0:T(8,128)(2,1)S(1)}, u32[]{:S(2)}, u32[]{:S(2)}) %collective-permute-start.4) | collective-permute-done | bytes 540704 | tf_op jit(solution)/shard_map/ppermute | solution.py:140
  59.7 0.1 convert_element_type.53.refs_0_
  59.7 1.7 %x_sum.3 = f32[16,16,1152]{2,1,0:T(8,128)S(1)} custom-call(f32[4,264,1024]{2,1,0:T(8,128)} %gram.3.own_ref, f32[264,1024]{1,0:T(8,128)S(1)} %convert_element_type.53.refs_0_, f32[264,1024]{1,0:T(8,128)S(1)} %convert_element_type.55.refs_1_, f32[264,1024]{1,0:T(8,128)S(1)} %convert_element_type.57.refs_2_), custom_call_target="tpu_custom_call" | custom-call | flops 2097152 | bytes 5242880 | tf_op jit(solution)/shard_map/x_sum/pallas_call | solution.py:91
  61.5 0.1 convert_bitcast_fusion
  61.6 0.3 pad_maximum_fusion
  61.9 42.8 %all_to_all.5 = f16[16,2,16,1152]{3,2,1,0:T(8,128)(2,1)S(1)} all-to-all(f16[16,2,16,1152]{3,2,1,0:T(8,128)(2,1)S(1)} %pad_maximum_fusion), channel_id=1, replica_groups=mesh['yh'=2,'z'=8,'x'=4,'yl'=2,'core'=2] {'yh','z'}, dimensions={0} | all-to-all | bytes 2359296 | tf_op jit(solution)/shard_map/all_to_all | solution.py:144
  104.6 0.2 convert_element_type.58.got_ref
  104.9 0.9 yz_sum.1
  (5 shorter events, 0.0 us)
Async XLA Ops:
  0.0 18.3 %collective-permute-start.3 = (bf16[768,1024]{1,0:T(8,128)(2,1)}, bf16[768,1024]{1,0:T(8,128)(2,1)S(1)}, u32[]{:S(2)}, u32[]{:S(2)}) collective-permute-start(bf16[768,1024]{1,0:T(8,128)(2,1)} %own_ref.3), channel_id=1, source_target_pairs={{0,3},{1,0},{2,1},{3,2},{4,7},{5,4},{6,5},{7,6},{8,11},{9,8},{10,9... | collective-permute-start | bytes 4718600 | tf_op jit(solution)/shard_map/ppermute | solution.py:133
  0.0 1.4 %copy-start.1 = (bf16[768,1024]{1,0:T(8,128)(2,1)S(1)}, bf16[768,1024]{1,0:T(8,128)(2,1)}, u32[]{:S(2)}) copy-start(bf16[768,1024]{1,0:T(8,128)(2,1)} %own_ref.3) | copy-start | bytes 4718596
  3.7 2.1 %copy-start = (f32[4,264,1024]{2,1,0:T(8,128)}, f32[4,264,1024]{2,1,0:T(8,128)S(1)}, u32[]{:S(2)}) copy-start(f32[4,264,1024]{2,1,0:T(8,128)S(1)} %gram.2.own_ref) | copy-start | bytes 12976132
  6.2 26.9 %collective-permute-start.2 = (f16[264,1024]{1,0:T(8,128)(2,1)S(1)}, f16[264,1024]{1,0:T(8,128)(2,1)S(1)}, u32[]{:S(2)}, u32[]{:S(2)}) collective-permute-start(f16[264,1024]{1,0:T(8,128)(2,1)S(1)} %get-tuple-element.5), channel_id=1, source_target_pairs={{0,12},{4,0},{8,4},{12,8},{1,13},{5,1},{9,5},{13,9},{2,14},{6,2},{... | collective-permute-start | bytes 1622024 | tf_op jit(solution)/shard_map/ppermute | solution.py:140
  9.0 24.1 %collective-permute-start.1 = (f16[264,1024]{1,0:T(8,128)(2,1)S(1)}, f16[264,1024]{1,0:T(8,128)(2,1)S(1)}, u32[]{:S(2)}, u32[]{:S(2)}) collective-permute-start(f16[264,1024]{1,0:T(8,128)(2,1)S(1)} %get-tuple-element.6), channel_id=1, source_target_pairs={{0,8},{4,12},{8,0},{12,4},{1,9},{5,13},{9,1},{13,5},{2,10},{6,14},... | collective-permute-start | bytes 1622024 | tf_op jit(solution)/shard_map/ppermute | solution.py:140
  9.8 27.4 %collective-permute-start = (f16[264,1024]{1,0:T(8,128)(2,1)S(1)}, f16[264,1024]{1,0:T(8,128)(2,1)S(1)}, u32[]{:S(2)}, u32[]{:S(2)}) collective-permute-start(f16[264,1024]{1,0:T(8,128)(2,1)S(1)} %get-tuple-element.7), channel_id=1, source_target_pairs={{0,4},{4,8},{8,12},{12,0},{1,5},{5,9},{9,13},{13,1},{2,6},{6,10},{... | collective-permute-start | bytes 1622024 | tf_op jit(solution)/shard_map/ppermute | solution.py:140
  25.6 30.4 %collective-permute-start.6 = (f16[264,1024]{1,0:T(8,128)(2,1)S(1)}, f16[264,1024]{1,0:T(8,128)(2,1)S(1)}, u32[]{:S(2)}, u32[]{:S(2)}) collective-permute-start(f16[264,1024]{1,0:T(8,128)(2,1)S(1)} %get-tuple-element.8), channel_id=1, source_target_pairs={{0,12},{4,0},{8,4},{12,8},{1,13},{5,1},{9,5},{13,9},{2,14},{6,2},{... | collective-permute-start | bytes 1622024 | tf_op jit(solution)/shard_map/ppermute | solution.py:140
  28.5 27.6 %collective-permute-start.5 = (f16[264,1024]{1,0:T(8,128)(2,1)S(1)}, f16[264,1024]{1,0:T(8,128)(2,1)S(1)}, u32[]{:S(2)}, u32[]{:S(2)}) collective-permute-start(f16[264,1024]{1,0:T(8,128)(2,1)S(1)} %get-tuple-element.9), channel_id=1, source_target_pairs={{0,8},{4,12},{8,0},{12,4},{1,9},{5,13},{9,1},{13,5},{2,10},{6,14},... | collective-permute-start | bytes 1622024 | tf_op jit(solution)/shard_map/ppermute | solution.py:140
  33.1 26.6 %collective-permute-start.4 = (f16[264,1024]{1,0:T(8,128)(2,1)S(1)}, f16[264,1024]{1,0:T(8,128)(2,1)S(1)}, u32[]{:S(2)}, u32[]{:S(2)}) collective-permute-start(f16[264,1024]{1,0:T(8,128)(2,1)S(1)} %get-tuple-element.10), channel_id=1, source_target_pairs={{0,4},{4,8},{8,12},{12,0},{1,5},{5,9},{9,13},{13,1},{2,6},{6,10},{... | collective-permute-start | bytes 1622024 | tf_op jit(solution)/shard_map/ppermute | solution.py:140

commit v2 on v0

v2 whole, which is shorter than its diff:
```python
import functools

import jax
import jax.numpy as jnp
from jax import lax
from jax.experimental import pallas as pl
from jax.experimental.pallas import tpu as pltpu
from jax.sharding import Mesh, PartitionSpec as P

SIZES = {"yh": 2, "z": 8, "x": 4, "yl": 2, "core": 2}
DP = ("yh", "z", "x")
FACTOR = ("yl", "core")
NX, NY, NZ = SIZES["x"], SIZES["yh"], SIZES["z"]
NF = SIZES["yl"] * SIZES["core"]
TOP = 15.0
VMEM = 48 * 1024 * 1024
CHUNK = 256


def share(index, count):
    return 1.0 - 0.5 * jnp.float32(index) / count


def lifted(power, factor):
    return jnp.max(jnp.exp2(jnp.full((8, 128), TOP - power))) * factor


def lowered(power, factor):
    return jnp.max(jnp.exp2(jnp.full((8, 128), power - TOP))) / factor


def ahead(axis, by):
    count = SIZES[axis]
    return lax.rem(lax.axis_index(axis) + by + count, count)


def sum_of(terms):
    return functools.reduce(lambda a, b: a + b, terms)


def rows_of(start, count):
    return pl.ds(pl.multiple_of(start, 16), count)


def senders(axis, blocks, growth):
    powers = [jnp.max(block[block.shape[0] - 8 :, :128]) for block in blocks]
    weights = [lowered(p, share(ahead(axis, -by), SIZES[axis])) for by, p in enumerate(powers)]
    return weights, functools.reduce(jnp.maximum, powers) + growth


def products(own_ref, partner_ref, visit):
    tokens, panel = own_ref.shape
    rows = panel // (NX * NY * NZ)
    largest = lambda ref: jnp.max(jnp.abs(ref[...]).astype(jnp.float32))
    bound = tokens * (largest(own_ref) + 1e-15) * (largest(partner_ref) + 1e-15)
    power = jnp.max(jnp.ceil(jnp.log2(jnp.full((8, 128), bound))))
    up = lifted(power, 1.0)
    for c in range(panel // CHUNK):
        product = lax.dot_general(
            own_ref[:, c * CHUNK : (c + 1) * CHUNK], partner_ref[...], (((0,), (0,)), ((), ())),
            preferred_element_type=jnp.float32,
        ) * up
        for n in range(CHUNK // rows):
            yz, x = divmod(c * (CHUNK // rows) + n, NX)
            visit(x, yz // NZ, yz % NZ, product[n * rows : (n + 1) * rows])
    return power


def diagonal_kernel(own_ref, partner_ref, out_ref):
    factor = share(lax.axis_index("x"), NX)

    def visit(x, y, z, value):
        rows = value.shape[0]
        to_x = lax.rem(x - lax.axis_index("x") + NX, NX)
        out_ref[to_x, rows_of((y * NZ + z) * rows, rows), :] = value * factor

    power = products(own_ref, partner_ref, visit)
    out_ref[:, out_ref.shape[1] - 8 :, :] = jnp.full((NX, 8, out_ref.shape[2]), power)


def beside_kernel(own_ref, partner_ref, left_ref, right_ref):
    half = left_ref.shape[2]
    by_y, by_x = share(lax.axis_index("yh"), NY), share(lax.axis_index("x"), NX)

    def visit(x, y, z, value):
        rows = value.shape[0]
        to_x = lax.rem(x - lax.axis_index("x") + NX, NX)
        to_y = lax.rem(y - lax.axis_index("yh") + NY, NY)
        left_ref[to_y, rows_of((to_x * NZ + z) * rows, rows), :] = value[:, :half] * by_y
        right_ref[to_x, rows_of((y * NZ + z) * rows, rows), :] = value[:, half:] * by_x

    power = products(own_ref, partner_ref, visit)
    left_ref[:, left_ref.shape[1] - 8 :, :] = jnp.full((NY, 8, half), power)
    right_ref[:, right_ref.shape[1] - 8 :, :] = jnp.full((NX, 8, half), power)


def x_to_y_kernel(own_ref, *refs):
    out_ref = refs[-1]
    blocks = [own_ref.at[0], *refs[:-1]]
    weights, power = senders("x", blocks, 2.0)
    up = lifted(power, share(lax.axis_index("yh"), NY))
    count = out_ref.shape[1] - 8
    for by in range(NY):
        part = rows_of(ahead("yh", by) * count, count)
        out_ref[by, :count, :] = sum_of([block[part, :] * (w * up) for block, w in zip(blocks, weights)])
    out_ref[:, count:, :] = jnp.full((NY, 8, out_ref.shape[2]), power)


def y_to_x_kernel(own_ref, got_ref, out_ref):
    blocks = [own_ref.at[0], got_ref]
    weights, power = senders("yh", blocks, 1.0)
    up = lifted(power, share(lax.axis_index("x"), NX))
    count = out_ref.shape[1] - 8
    for by in range(NX):
        part = pl.ds(by * count, count)
        out_ref[by, :count, :] = sum_of([block[part, :] * (w * up) for block, w in zip(blocks, weights)])
    out_ref[:, count:, :] = jnp.full((NX, 8, out_ref.shape[2]), power)


def to_z_kernel(*refs):
    first, right, left, out_ref = refs[:NY], refs[NY : 2 * NY], refs[2 * NY : -1], refs[-1]
    first, right, left = ([group[0].at[0], *group[1:]] for group in (first, right, left))
    w_first, p_first = senders("yh", first, 1.0)
    w_right, p_right = senders("yh", right, 1.0)
    w_left, p_left = senders("x", left, 2.0)
    power = jnp.maximum(p_first, jnp.maximum(p_right, p_left))
    up = lifted(power, share(lax.axis_index("z"), NZ))
    _, _, rows, wide = out_ref.shape
    panel = wide - 128
    half = panel // 2
    for z in range(NZ):
        part = pl.ds(z * rows, rows)
        total = lambda blocks, weights: sum_of([block[part, :] * (w * up) for block, w in zip(blocks, weights)])
        out_ref[z, 0, :, :panel] = total(first, w_first)
        out_ref[z, 1, :, :half] = total(left, w_left)
        out_ref[z, 1, :, half:panel] = total(right, w_right)
    out_ref[:, :, :, panel:] = jnp.full((NZ, 2, rows, 128), power)


def z_sum_kernel(scale, got_ref, out_ref):
    panel = out_ref.shape[2]
    for k in range(2):
        weights = [jnp.exp2(got_ref[s, k, :, panel:] - TOP) * (scale / float(1.0 - 0.5 * s / NZ)) for s in range(NZ)]
        for j in range(panel // 128):
            part = slice(j * 128, (j + 1) * 128)
            out_ref[k, :, part] = sum_of([got_ref[s, k, :, part] * w for s, w in enumerate(weights)])


def call(kernel, name, outs, *operands, flops=0):
    whole = lambda shape: pl.BlockSpec(shape, lambda i: (0,) * len(shape))
    arrays = [o[0] if isinstance(o, tuple) else o for o in operands]
    specs = [whole((1, *o[0].shape[1:]) if isinstance(o, tuple) else o.shape) for o in operands]
    out_shape = [jax.ShapeDtypeStruct(shape, jnp.float32) for shape in outs]
    moved = sum(a.size * a.dtype.itemsize for a in arrays) + sum(4 * s.size for s in out_shape)
    result = pl.pallas_call(
        kernel,
        grid=(1,),
        out_shape=out_shape,
        in_specs=specs,
        out_specs=[whole(s.shape) for s in out_shape],
        compiler_params=pltpu.CompilerParams(vmem_limit_bytes=VMEM),
        cost_estimate=pl.CostEstimate(flops=flops, bytes_accessed=moved, transcendentals=0),
        name=name,
    )(*arrays)
    return result if len(outs) > 1 else result[0]


def passed(value, axis, by):
    count = lax.axis_size(axis)
    return lax.ppermute(value, axis, [(i, (i + by) % count) for i in range(count)])


def per_device(acts):
    tokens, panel = acts.shape
    rows = panel // (NX * NY * NZ)
    half = panel // 2
    scale = 1.0 / (tokens * NX * NY * NZ)
    flops = 2 * tokens * panel * panel
    short = lambda value: value.astype(jnp.float16)
    long = lambda value: value.astype(jnp.float32)

    partner = passed(acts, FACTOR, NF - 1)

    first = call(diagonal_kernel, "diagonal", [(NX, NY * NZ * rows + 8, panel)], acts, acts, flops=flops)
    got_first = [passed(short(first[by]), "x", by) for by in range(1, NX)]

    left, right = call(
        beside_kernel, "beside", [(NY, NX * NZ * rows + 8, half), (NX, NY * NZ * rows + 8, half)], acts, partner,
        flops=flops,
    )
    left_sent, right_sent = short(left[1]), [short(right[by]) for by in range(1, NX)]
    got_left = passed(left_sent, "yh", 1)
    got_right = [passed(right_sent[by - 1], "x", by) for by in range(1, NX)]

    ahead_of = [long(jnp.concatenate([s, left_sent[: s.shape[0]]], axis=1)) for s in right_sent]
    got_first = [long(g) + 0.0 * s for g, s in zip(got_first, ahead_of)]

    lines = NZ * rows + 8
    first = call(x_to_y_kernel, "first_x", [(NY, lines, panel)], (first, 0), *got_first)
    got_first = passed(short(first[1]), "yh", 1)
    left = call(y_to_x_kernel, "left_y", [(NX, lines, half)], (left, 0), long(got_left))
    got_left = [passed(short(left[by]), "x", by) for by in range(1, NX)]
    right = call(x_to_y_kernel, "right_x", [(NY, lines, half)], (right, 0), *map(long, got_right))
    got_right = passed(short(right[1]), "yh", 1)

    sent = call(
        to_z_kernel, "to_z", [(NZ, 2, rows, panel + 128)],
        (first, 0), long(got_first), (right, 0), long(got_right), (left, 0), *map(long, got_left),
    )
    got = lax.all_to_all(short(sent), "z", 0, 0, tiled=True)
    return call(functools.partial(z_sum_kernel, scale), "z_sum", [(2, rows, panel)], long(got))


def solution(mesh):
    fine = Mesh(mesh.devices.reshape(tuple(SIZES.values())), tuple(SIZES))
    return jax.shard_map(
        per_device,
        mesh=fine,
        in_specs=(P(DP, FACTOR),),
        out_specs=P(None, FACTOR + DP, None),
        check_vma=False,
    )
```

time: 421 us -> 89.9 us (0.21)
  waiting for transfers between devices: 398 us -> 24.8 us
  blocking collectives: 0 us -> 26.8 us
  starting transfers between devices: 0.01 us -> 21.9 us
  between operations: 13.4 us -> 0.23 us
  Pallas kernels: 0 us -> 9.81 us
  matrix products: 5.79 us -> 0 us
    reduce_scatter x1 -> x0, waiting for transfers between devices: 383 us -> none  [per_device(): summed = lax.psum_scatter(whole, 'dp', scatter_dimension=1, tiled=True)]
    all_to_all x0 -> x1, blocking collectives: none -> 26.8 us  [per_device(): got = lax.all_to_all(short(sent), 'z', 0, 0, tiled=True)]
    ppermute x1 -> x13, starting transfers between devices: 0.01 us -> 21.9 us  [passed(): lax.ppermute(value, axis, [(i, (i + by) % count) for i in range(count)])]
    ppermute x1 -> x13, waiting for transfers between devices: 14.4 us -> 24.8 us  [passed(): lax.ppermute(value, axis, [(i, (i + by) % count) for i in range(count)])]
    pallas_call x0 -> x7, Pallas kernels: none -> 9.81 us  [call(): pl.pallas_call(kernel, grid=(1,), out_shape=out_shape, in_specs=specs, ou...]
    dot_general x2 -> x0, matrix products: 5.79 us -> none  [block_rows(): jnp.einsum('tc,tj->cj', own, partner, preferred_element_type=jnp.float32)]
  transfers between devices with their start and end apart: 2 -> 13, of which waited for: 2 -> 8; matrix products, arithmetic and copies ran while one was open for 1% -> 3% of each run, Pallas kernels for 0% -> 10%
where the time goes in v2:
time: 89.9 us; the launch traced here: 89.7 us
  blocking collectives  26.8 us (30%)
  waiting for transfers between devices  24.8 us (28%)
  starting transfers between devices  21.9 us (24%)
  Pallas kernels  9.81 us (11%)
  local copies, waits for them, and re-layouts  3.85 us (4%)
  other arithmetic  2.26 us (3%)
    all_to_all x1, blocking collectives, per_device(): got = lax.all_to_all(short(sent), 'z', 0, 0, tiled=True)  26.8 us
    ppermute x13, waiting for transfers between devices, passed(): lax.ppermute(value, axis, [(i, (i + by) % count) for i in range(count)])  24.8 us
    ppermute x13, starting transfers between devices, passed(): lax.ppermute(value, axis, [(i, (i + by) % count) for i in range(count)])  21.9 us
    pallas_call x7, Pallas kernels, call(): pl.pallas_call(kernel, grid=(1,), out_shape=out_shape, in_specs=specs, ou...  9.81 us
    unnamed x8, local copies, waits for them, and re-layouts  3 us
  transfers between devices with their start and end apart: 13, of which 8 were waited for; matrix products, arithmetic and copies ran while one was open for 3% of the time, Pallas kernels for 10%

profile of v2, /device:TPU:8, one launch (start us, length us, event | category | flops | bytes accessed | tf_op | source)
XLA Modules:
  0.0 89.7 jit_solution(7781833519570601443)
XLA Ops:
  0.0 1.4 %copy-done.2 = bf16[768,1024]{1,0:T(8,128)(2,1)S(1)} copy-done((bf16[768,1024]{1,0:T(8,128)(2,1)S(1)}, bf16[768,1024]{1,0:T(8,128)(2,1)}, u32[]{:S(2)}) %copy-start.2) | copy-done | bytes 1572888
  1.4 2.3 %diagonal.1.own_ref = f32[4,264,1024]{2,1,0:T(8,128)S(1)} custom-call(bf16[768,1024]{1,0:T(8,128)(2,1)S(1)} %copy-done.2, bf16[768,1024]{1,0:T(8,128)(2,1)S(1)} %copy-done.2), custom_call_target="tpu_custom_call" | custom-call | flops 1610612736 | bytes 7471104 | tf_op jit(solution)/shard_map/diagonal/pallas_call | solution.py:155
  3.8 0.4 convert.24
  4.2 1.6 %copy-done = f32[4,264,1024]{2,1,0:T(8,128)} copy-done((f32[4,264,1024]{2,1,0:T(8,128)}, f32[4,264,1024]{2,1,0:T(8,128)S(1)}, u32[]{:S(2)}) %copy-start) | copy-done | bytes 4325400
  5.7 0.5 slice_bitcast_fusion
  6.2 2.8 %collective-permute-start.3 = (f16[264,1024]{1,0:T(8,128)(2,1)S(1)}, f16[264,1024]{1,0:T(8,128)(2,1)S(1)}, u32[]{:S(2)}, u32[]{:S(2)}) collective-permute-start(f16[264,1024]{1,0:T(8,128)(2,1)S(1)} %get-tuple-element.9), channel_id=1, source_target_pairs={{0,12},{4,0},{8,4},{12,8},{1,13},{5,1},{9,5},{13,9},{2,14},{6,2},{... | collective-permute-start | bytes 1622024 | tf_op jit(solution)/shard_map/ppermute | solution.py:170
  9.0 0.8 collective-permute-start.2
  9.9 0.9 collective-permute-start
  10.7 7.5 %collective-permute-done.1.partner_ref = bf16[768,1024]{1,0:T(8,128)(2,1)S(1)} collective-permute-done((bf16[768,1024]{1,0:T(8,128)(2,1)}, bf16[768,1024]{1,0:T(8,128)(2,1)S(1)}, u32[]{:S(2)}, u32[]{:S(2)}) %collective-permute-start.1) | collective-permute-done | bytes 1572896 | tf_op jit(solution)/shard_map/ppermute | solution.py:170
  18.3 3.7 %beside.1 = (f32[2,520,512]{2,1,0:T(8,128)S(1)}, f32[4,264,512]{2,1,0:T(8,128)}) custom-call(bf16[768,1024]{1,0:T(8,128)(2,1)S(1)} %copy-done.3, bf16[768,1024]{1,0:T(8,128)(2,1)S(1)} %collective-permute-done.1.partner_ref), custom_call_target="tpu_custom_call" | custom-call | flops 1610612736 | bytes 7438336 | tf_op jit(solution)/shard_map/beside/pallas_call | solution.py:155
  22.3 2.6 %collective-permute-start.9 = (f16[520,512]{1,0:T(8,128)(2,1)S(1)}, f16[520,512]{1,0:T(8,128)(2,1)S(1)}, u32[]{:S(2)}, u32[]{:S(2)}) collective-permute-start(f16[520,512]{1,0:T(8,128)(2,1)S(1)} %slice_bitcast_fusion.3), channel_id=1, source_target_pairs={{0,128},{128,0},{1,129},{129,1},{2,130},{130,2},{3,131},{131,3},{4... | collective-permute-start | bytes 1597448 | tf_op jit(solution)/shard_map/ppermute | solution.py:170
  25.3 2.8 %collective-permute-start.7 = (f16[264,512]{1,0:T(8,128)(2,1)S(1)}, f16[264,512]{1,0:T(8,128)(2,1)S(1)}, u32[]{:S(2)}, u32[]{:S(2)}) collective-permute-start(f16[264,512]{1,0:T(8,128)(2,1)S(1)} %get-tuple-element.12), channel_id=1, source_target_pairs={{0,12},{4,0},{8,4},{12,8},{1,13},{5,1},{9,5},{13,9},{2,14},{6,2},{... | collective-permute-start | bytes 811016 | tf_op jit(solution)/shard_map/ppermute | solution.py:170
  28.2 4.9 %collective-permute-done.3 = f16[264,1024]{1,0:T(8,128)(2,1)S(1)} collective-permute-done((f16[264,1024]{1,0:T(8,128)(2,1)S(1)}, f16[264,1024]{1,0:T(8,128)(2,1)S(1)}, u32[]{:S(2)}, u32[]{:S(2)}) %collective-permute-start.3) | collective-permute-done | bytes 540704 | tf_op jit(solution)/shard_map/ppermute | solution.py:170
  33.1 4.7 %collective-permute-start.5 = (f16[264,512]{1,0:T(8,128)(2,1)S(1)}, f16[264,512]{1,0:T(8,128)(2,1)S(1)}, u32[]{:S(2)}, u32[]{:S(2)}) collective-permute-start(f16[264,512]{1,0:T(8,128)(2,1)S(1)} %get-tuple-element.14), channel_id=1, source_target_pairs={{0,4},{4,8},{8,12},{12,0},{1,5},{5,9},{9,13},{13,1},{2,6},{6,10},{... | collective-permute-start | bytes 811016 | tf_op jit(solution)/shard_map/ppermute | solution.py:170
  37.8 0.6 multiply_add_fusion
  38.4 1.9 %first_x.1.refs_0_ = f32[2,136,1024]{2,1,0:T(8,128)S(1)} custom-call(f32[4,264,1024]{2,1,0:T(8,128)} %copy-done, f32[264,1024]{1,0:T(8,128)S(1)} %get-tuple-element.20.refs_0_, f32[264,1024]{1,0:T(8,128)S(1)} %get-tuple-element.19.refs_1_, f32[264,1024]{1,0:T(8,128)S(1)} %get-tuple-element.18.refs_2_), custom_call_target="tpu_custom_call" | custom-call | bytes 8683520 | tf_op jit(solution)/shard_map/first_x/pallas_call | solution.py:155
  40.4 2.6 %collective-permute-start.4 = (f16[136,1024]{1,0:T(8,128)(2,1)S(1)}, f16[136,1024]{1,0:T(8,128)(2,1)S(1)}, u32[]{:S(2)}, u32[]{:S(2)}) collective-permute-start(f16[136,1024]{1,0:T(8,128)(2,1)S(1)} %fusion), channel_id=1, source_target_pairs={{0,128},{128,0},{1,129},{129,1},{2,130},{130,2},{3,131},{131,3},{4... | collective-permute-start | bytes 835592 | tf_op jit(solution)/shard_map/ppermute | solution.py:170
  43.0 1.5 %collective-permute-done.7 = f16[264,512]{1,0:T(8,128)(2,1)S(1)} collective-permute-done((f16[264,512]{1,0:T(8,128)(2,1)S(1)}, f16[264,512]{1,0:T(8,128)(2,1)S(1)}, u32[]{:S(2)}, u32[]{:S(2)}) %collective-permute-start.7) | collective-permute-done | bytes 270368 | tf_op jit(solution)/shard_map/ppermute | solution.py:170
  44.6 3.6 %collective-permute-done.5 = f16[264,512]{1,0:T(8,128)(2,1)S(1)} collective-permute-done((f16[264,512]{1,0:T(8,128)(2,1)S(1)}, f16[264,512]{1,0:T(8,128)(2,1)S(1)}, u32[]{:S(2)}, u32[]{:S(2)}) %collective-permute-start.5) | collective-permute-done | bytes 270368 | tf_op jit(solution)/shard_map/ppermute | solution.py:170
  48.2 0.4 right_x.1.refs_2_
  48.7 2.3 %collective-permute-start.8 = (f16[136,512]{1,0:T(8,128)(2,1)S(1)}, f16[136,512]{1,0:T(8,128)(2,1)S(1)}, u32[]{:S(2)}, u32[]{:S(2)}) collective-permute-start(f16[136,512]{1,0:T(8,128)(2,1)S(1)} %fusion.1), channel_id=1, source_target_pairs={{0,128},{128,0},{1,129},{129,1},{2,130},{130,2},{3,131},{131,3},{4... | collective-permute-start | bytes 417800 | tf_op jit(solution)/shard_map/ppermute | solution.py:170
  51.1 0.4 left_y.1.refs_4_
  51.7 0.7 collective-permute-start.12
  52.4 0.8 collective-permute-start.11
  53.2 0.8 collective-permute-start.10
  54.1 1.8 %collective-permute-done.8 = f16[136,512]{1,0:T(8,128)(2,1)S(1)} collective-permute-done((f16[136,512]{1,0:T(8,128)(2,1)S(1)}, f16[136,512]{1,0:T(8,128)(2,1)S(1)}, u32[]{:S(2)}, u32[]{:S(2)}) %collective-permute-start.8) | collective-permute-done | bytes 139296 | tf_op jit(solution)/shard_map/ppermute | solution.py:170
  55.9 2.5 %collective-permute-done.12 = f16[136,512]{1,0:T(8,128)(2,1)S(1)} collective-permute-done((f16[136,512]{1,0:T(8,128)(2,1)S(1)}, f16[136,512]{1,0:T(8,128)(2,1)S(1)}, u32[]{:S(2)}, u32[]{:S(2)}) %collective-permute-start.12) | collective-permute-done | bytes 139296 | tf_op jit(solution)/shard_map/ppermute | solution.py:170
  58.4 2.0 %collective-permute-done.11 = f16[136,512]{1,0:T(8,128)(2,1)S(1)} collective-permute-done((f16[136,512]{1,0:T(8,128)(2,1)S(1)}, f16[136,512]{1,0:T(8,128)(2,1)S(1)}, u32[]{:S(2)}, u32[]{:S(2)}) %collective-permute-start.11) | collective-permute-done | bytes 139296 | tf_op jit(solution)/shard_map/ppermute | solution.py:170
  60.4 1.1 %collective-permute-done.10 = f16[136,512]{1,0:T(8,128)(2,1)S(1)} collective-permute-done((f16[136,512]{1,0:T(8,128)(2,1)S(1)}, f16[136,512]{1,0:T(8,128)(2,1)S(1)}, u32[]{:S(2)}, u32[]{:S(2)}) %collective-permute-start.10) | collective-permute-done | bytes 139296 | tf_op jit(solution)/shard_map/ppermute | solution.py:170
  61.6 0.4 to_z.1
  62.1 26.8 %all_to_all.5 = f16[8,2,16,1152]{3,2,1,0:T(8,128)(2,1)S(1)} all-to-all(f16[8,2,16,1152]{3,2,1,0:T(8,128)(2,1)S(1)} %convert_element_type.126), channel_id=1, replica_groups=mesh['yh'=2,'z'=8,'x'=4,'yl'=2,'core'=2] {'z'}, dimensions={0} | all-to-all | bytes 1179648 | tf_op jit(solution)/shard_map/all_to_all | solution.py:210
  88.9 0.7 z_sum.1
  (33 shorter events, 1.7 us)
Async XLA Ops:
  0.0 18.3 %collective-permute-start.1 = (bf16[768,1024]{1,0:T(8,128)(2,1)}, bf16[768,1024]{1,0:T(8,128)(2,1)S(1)}, u32[]{:S(2)}, u32[]{:S(2)}) collective-permute-start(bf16[768,1024]{1,0:T(8,128)(2,1)} %own_ref.3), channel_id=1, source_target_pairs={{0,3},{1,0},{2,1},{3,2},{4,7},{5,4},{6,5},{7,6},{8,11},{9,8},{10,9... | collective-permute-start | bytes 4718600 | tf_op jit(solution)/shard_map/ppermute | solution.py:170
  0.0 1.4 %copy-start.2 = (bf16[768,1024]{1,0:T(8,128)(2,1)S(1)}, bf16[768,1024]{1,0:T(8,128)(2,1)}, u32[]{:S(2)}) copy-start(bf16[768,1024]{1,0:T(8,128)(2,1)} %own_ref.3) | copy-start | bytes 4718596
  3.7 2.0 %copy-start = (f32[4,264,1024]{2,1,0:T(8,128)}, f32[4,264,1024]{2,1,0:T(8,128)S(1)}, u32[]{:S(2)}) copy-start(f32[4,264,1024]{2,1,0:T(8,128)S(1)} %diagonal.1.own_ref) | copy-start | bytes 12976132
  5.7 12.5 %copy-start.3 = (bf16[768,1024]{1,0:T(8,128)(2,1)S(1)}, bf16[768,1024]{1,0:T(8,128)(2,1)}, u32[]{:S(2)}) copy-start(bf16[768,1024]{1,0:T(8,128)(2,1)} %own_ref.3) | copy-start | bytes 4718596
  6.2 26.9 %collective-permute-start.3 = (f16[264,1024]{1,0:T(8,128)(2,1)S(1)}, f16[264,1024]{1,0:T(8,128)(2,1)S(1)}, u32[]{:S(2)}, u32[]{:S(2)}) collective-permute-start(f16[264,1024]{1,0:T(8,128)(2,1)S(1)} %get-tuple-element.9), channel_id=1, source_target_pairs={{0,12},{4,0},{8,4},{12,8},{1,13},{5,1},{9,5},{13,9},{2,14},{6,2},{... | collective-permute-start | bytes 1622024 | tf_op jit(solution)/shard_map/ppermute | solution.py:170
  9.0 24.0 %collective-permute-start.2 = (f16[264,1024]{1,0:T(8,128)(2,1)S(1)}, f16[264,1024]{1,0:T(8,128)(2,1)S(1)}, u32[]{:S(2)}, u32[]{:S(2)}) collective-permute-start(f16[264,1024]{1,0:T(8,128)(2,1)S(1)} %get-tuple-element.10), channel_id=1, source_target_pairs={{0,8},{4,12},{8,0},{12,4},{1,9},{5,13},{9,1},{13,5},{2,10},{6,14},... | collective-permute-start | bytes 1622024 | tf_op jit(solution)/shard_map/ppermute | solution.py:170
  9.9 27.9 %collective-permute-start = (f16[264,1024]{1,0:T(8,128)(2,1)S(1)}, f16[264,1024]{1,0:T(8,128)(2,1)S(1)}, u32[]{:S(2)}, u32[]{:S(2)}) collective-permute-start(f16[264,1024]{1,0:T(8,128)(2,1)S(1)} %get-tuple-element.11), channel_id=1, source_target_pairs={{0,4},{4,8},{8,12},{12,0},{1,5},{5,9},{9,13},{13,1},{2,6},{6,10},{... | collective-permute-start | bytes 1622024 | tf_op jit(solution)/shard_map/ppermute | solution.py:170
  21.9 2.9 %copy-start.1 = (f32[4,264,512]{2,1,0:T(8,128)S(1)}, f32[4,264,512]{2,1,0:T(8,128)}, u32[]{:S(2)}) copy-start(f32[4,264,512]{2,1,0:T(8,128)} %get-tuple-element.7.own_ref) | copy-start | bytes 6488068
  22.3 28.7 %collective-permute-start.9 = (f16[520,512]{1,0:T(8,128)(2,1)S(1)}, f16[520,512]{1,0:T(8,128)(2,1)S(1)}, u32[]{:S(2)}, u32[]{:S(2)}) collective-permute-start(f16[520,512]{1,0:T(8,128)(2,1)S(1)} %slice_bitcast_fusion.3), channel_id=1, source_target_pairs={{0,128},{128,0},{1,129},{129,1},{2,130},{130,2},{3,131},{131,3},{4... | collective-permute-start | bytes 1597448 | tf_op jit(solution)/shard_map/ppermute | solution.py:170
  25.3 19.1 %collective-permute-start.7 = (f16[264,512]{1,0:T(8,128)(2,1)S(1)}, f16[264,512]{1,0:T(8,128)(2,1)S(1)}, u32[]{:S(2)}, u32[]{:S(2)}) collective-permute-start(f16[264,512]{1,0:T(8,128)(2,1)S(1)} %get-tuple-element.12), channel_id=1, source_target_pairs={{0,12},{4,0},{8,4},{12,8},{1,13},{5,1},{9,5},{13,9},{2,14},{6,2},{... | collective-permute-start | bytes 811016 | tf_op jit(solution)/shard_map/ppermute | solution.py:170
  33.1 11.4 %collective-permute-start.6 = (f16[264,512]{1,0:T(8,128)(2,1)S(1)}, f16[264,512]{1,0:T(8,128)(2,1)S(1)}, u32[]{:S(2)}, u32[]{:S(2)}) collective-permute-start(f16[264,512]{1,0:T(8,128)(2,1)S(1)} %get-tuple-element.13), channel_id=1, source_target_pairs={{0,8},{4,12},{8,0},{12,4},{1,9},{5,13},{9,1},{13,5},{2,10},{6,14},... | collective-permute-start | bytes 811016 | tf_op jit(solution)/shard_map/ppermute | solution.py:170
  33.1 15.1 %collective-permute-start.5 = (f16[264,512]{1,0:T(8,128)(2,1)S(1)}, f16[264,512]{1,0:T(8,128)(2,1)S(1)}, u32[]{:S(2)}, u32[]{:S(2)}) collective-permute-start(f16[264,512]{1,0:T(8,128)(2,1)S(1)} %get-tuple-element.14), channel_id=1, source_target_pairs={{0,4},{4,8},{8,12},{12,0},{1,5},{5,9},{9,13},{13,1},{2,6},{6,10},{... | collective-permute-start | bytes 811016 | tf_op jit(solution)/shard_map/ppermute | solution.py:170
  40.4 13.7 %collective-permute-start.4 = (f16[136,1024]{1,0:T(8,128)(2,1)S(1)}, f16[136,1024]{1,0:T(8,128)(2,1)S(1)}, u32[]{:S(2)}, u32[]{:S(2)}) collective-permute-start(f16[136,1024]{1,0:T(8,128)(2,1)S(1)} %fusion), channel_id=1, source_target_pairs={{0,128},{128,0},{1,129},{129,1},{2,130},{130,2},{3,131},{131,3},{4... | collective-permute-start | bytes 835592 | tf_op jit(solution)/shard_map/ppermute | solution.py:170
  48.7 7.2 %collective-permute-start.8 = (f16[136,512]{1,0:T(8,128)(2,1)S(1)}, f16[136,512]{1,0:T(8,128)(2,1)S(1)}, u32[]{:S(2)}, u32[]{:S(2)}) collective-permute-start(f16[136,512]{1,0:T(8,128)(2,1)S(1)} %fusion.1), channel_id=1, source_target_pairs={{0,128},{128,0},{1,129},{129,1},{2,130},{130,2},{3,131},{131,3},{4... | collective-permute-start | bytes 417800 | tf_op jit(solution)/shard_map/ppermute | solution.py:170
  51.7 6.7 %collective-permute-start.12 = (f16[136,512]{1,0:T(8,128)(2,1)S(1)}, f16[136,512]{1,0:T(8,128)(2,1)S(1)}, u32[]{:S(2)}, u32[]{:S(2)}) collective-permute-start(f16[136,512]{1,0:T(8,128)(2,1)S(1)} %get-tuple-element.15), channel_id=1, source_target_pairs={{0,12},{4,0},{8,4},{12,8},{1,13},{5,1},{9,5},{13,9},{2,14},{6,2},{... | collective-permute-start | bytes 417800 | tf_op jit(solution)/shard_map/ppermute | solution.py:170
  52.4 8.0 %collective-permute-start.11 = (f16[136,512]{1,0:T(8,128)(2,1)S(1)}, f16[136,512]{1,0:T(8,128)(2,1)S(1)}, u32[]{:S(2)}, u32[]{:S(2)}) collective-permute-start(f16[136,512]{1,0:T(8,128)(2,1)S(1)} %get-tuple-element.16), channel_id=1, source_target_pairs={{0,8},{4,12},{8,0},{12,4},{1,9},{5,13},{9,1},{13,5},{2,10},{6,14},... | collective-permute-start | bytes 417800 | tf_op jit(solution)/shard_map/ppermute | solution.py:170
  53.2 8.3 %collective-permute-start.10 = (f16[136,512]{1,0:T(8,128)(2,1)S(1)}, f16[136,512]{1,0:T(8,128)(2,1)S(1)}, u32[]{:S(2)}, u32[]{:S(2)}) collective-permute-start(f16[136,512]{1,0:T(8,128)(2,1)S(1)} %get-tuple-element.17), channel_id=1, source_target_pairs={{0,4},{4,8},{8,12},{12,0},{1,5},{5,9},{9,13},{13,1},{2,6},{6,10},{... | collective-permute-start | bytes 417800 | tf_op jit(solution)/shard_map/ppermute | solution.py:170

commit v3 on v2

--- a/solution.py
+++ b/solution.py
@@ -13,7 +13,7 @@
 NX, NY, NZ = SIZES["x"], SIZES["yh"], SIZES["z"]
 NF = SIZES["yl"] * SIZES["core"]
 TOP = 15.0
-VMEM = 48 * 1024 * 1024
+VMEM = 20 * 1024 * 1024
 CHUNK = 256
 
 
@@ -199,8 +199,11 @@
     first = call(x_to_y_kernel, "first_x", [(NY, lines, panel)], (first, 0), *got_first)
     got_first = passed(short(first[1]), "yh", 1)
     left = call(y_to_x_kernel, "left_y", [(NX, lines, half)], (left, 0), long(got_left))
-    got_left = [passed(short(left[by]), "x", by) for by in range(1, NX)]
-    right = call(x_to_y_kernel, "right_x", [(NY, lines, half)], (right, 0), *map(long, got_right))
+    left_sent = [short(left[by]) for by in range(1, NX)]
+    got_left = [passed(s, "x", by) for by, s in enumerate(left_sent, 1)]
+    ahead_of = [long(jnp.concatenate([s, s], axis=0)[: g.shape[0]]) for s, g in zip(left_sent, got_right)]
+    got_right = [long(g) + 0.0 * s for g, s in zip(got_right, ahead_of)]
+    right = call(x_to_y_kernel, "right_x", [(NY, lines, half)], (right, 0), *got_right)
     got_right = passed(short(right[1]), "yh", 1)
 
     sent = call(

time: 89.9 us -> 82.3 us (0.915)
  waiting for transfers between devices: 24.8 us -> 19.9 us
  starting transfers between devices: 21.9 us -> 24.7 us
  Pallas kernels: 9.81 us -> 7.17 us
  blocking collectives: 26.8 us -> 24.9 us
  local copies, waits for them, and re-layouts: 3.85 us -> 2.24 us
    ppermute x13, waiting for transfers between devices: 24.8 us -> 19.9 us  [passed(): lax.ppermute(value, axis, [(i, (i + by) % count) for i in range(count)])]
    ppermute x13, starting transfers between devices: 21.9 us -> 24.7 us  [passed(): lax.ppermute(value, axis, [(i, (i + by) % count) for i in range(count)])]
    pallas_call x7, Pallas kernels: 9.81 us -> 7.17 us  [call(): pl.pallas_call(kernel, grid=(1,), out_shape=out_shape, in_specs=specs, ou...]
    all_to_all x1, blocking collectives: 26.8 us -> 24.9 us  [per_device(): got = lax.all_to_all(short(sent), 'z', 0, 0, tiled=True)]
    unnamed x8 -> x4, local copies, waits for them, and re-layouts: 3 us -> 1.45 us
  transfers between devices with their start and end apart: 13 -> 13, of which waited for: 8 -> 5; matrix products, arithmetic and copies ran while one was open for 3% -> 4% of each run, Pallas kernels for 10% -> 7%
where the time goes in v3:
time: 82.3 us; the launch traced here: 81.4 us
  blocking collectives  24.9 us (30%)
  starting transfers between devices  24.7 us (30%)
  waiting for transfers between devices  19.9 us (24%)
  Pallas kernels  7.17 us (9%)
  other arithmetic  2.35 us (3%)
  local copies, waits for them, and re-layouts  2.24 us (3%)
    all_to_all x1, blocking collectives, per_device(): got = lax.all_to_all(short(sent), 'z', 0, 0, tiled=True)  24.9 us
    ppermute x13, starting transfers between devices, passed(): lax.ppermute(value, axis, [(i, (i + by) % count) for i in range(count)])  24.7 us
    ppermute x13, waiting for transfers between devices, passed(): lax.ppermute(value, axis, [(i, (i + by) % count) for i in range(count)])  19.9 us
    pallas_call x7, Pallas kernels, call(): pl.pallas_call(kernel, grid=(1,), out_shape=out_shape, in_specs=specs, ou...  7.17 us
  transfers between devices with their start and end apart: 13, of which 5 were waited for; matrix products, arithmetic and copies ran while one was open for 4% of the time, Pallas kernels for 7%

profile of v3, /device:TPU:8, one launch (start us, length us, event | category | flops | bytes accessed | tf_op | source)
XLA Modules:
  0.0 81.4 jit_solution(808903482236518734)
XLA Ops:
  0.0 1.4 %copy-done = bf16[768,1024]{1,0:T(8,128)(2,1)S(1)} copy-done((bf16[768,1024]{1,0:T(8,128)(2,1)S(1)}, bf16[768,1024]{1,0:T(8,128)(2,1)}, u32[]{:S(2)}) %copy-start) | copy-done | bytes 1572888
  1.4 2.3 %diagonal.1.own_ref = f32[4,264,1024]{2,1,0:T(8,128)S(1)} custom-call(bf16[768,1024]{1,0:T(8,128)(2,1)S(1)} %copy-done, bf16[768,1024]{1,0:T(8,128)(2,1)S(1)} %copy-done), custom_call_target="tpu_custom_call" | custom-call | flops 1610612736 | bytes 7471104 | tf_op jit(solution)/shard_map/diagonal/pallas_call | solution.py:155
  3.7 0.4 convert.24
  4.2 0.4 slice_bitcast_fusion
  4.6 2.8 %collective-permute-start.3 = (f16[264,1024]{1,0:T(8,128)(2,1)S(1)}, f16[264,1024]{1,0:T(8,128)(2,1)S(1)}, u32[]{:S(2)}, u32[]{:S(2)}) collective-permute-start(f16[264,1024]{1,0:T(8,128)(2,1)S(1)} %get-tuple-element.9), channel_id=1, source_target_pairs={{0,12},{4,0},{8,4},{12,8},{1,13},{5,1},{9,5},{13,9},{2,14},{6,2},{... | collective-permute-start | bytes 1622024 | tf_op jit(solution)/shard_map/ppermute | solution.py:170
  7.4 0.8 collective-permute-start.2
  8.3 0.9 %collective-permute-start = (f16[264,1024]{1,0:T(8,128)(2,1)S(1)}, f16[264,1024]{1,0:T(8,128)(2,1)S(1)}, u32[]{:S(2)}, u32[]{:S(2)}) collective-permute-start(f16[264,1024]{1,0:T(8,128)(2,1)S(1)} %get-tuple-element.11), channel_id=1, source_target_pairs={{0,4},{4,8},{8,12},{12,0},{1,5},{5,9},{9,13},{13,1},{2,6},{6,10},{... | collective-permute-start | bytes 1622024 | tf_op jit(solution)/shard_map/ppermute | solution.py:170
  9.1 9.1 %collective-permute-done.1.partner_ref = bf16[768,1024]{1,0:T(8,128)(2,1)S(1)} collective-permute-done((bf16[768,1024]{1,0:T(8,128)(2,1)}, bf16[768,1024]{1,0:T(8,128)(2,1)S(1)}, u32[]{:S(2)}, u32[]{:S(2)}) %collective-permute-start.1) | collective-permute-done | bytes 1572896 | tf_op jit(solution)/shard_map/ppermute | solution.py:170
  18.3 2.3 %beside.1 = (f32[2,520,512]{2,1,0:T(8,128)S(1)}, f32[4,264,512]{2,1,0:T(8,128)S(1)}) custom-call(bf16[768,1024]{1,0:T(8,128)(2,1)S(1)} %copy-done.1, bf16[768,1024]{1,0:T(8,128)(2,1)S(1)} %collective-permute-done.1.partner_ref), custom_call_target="tpu_custom_call" | custom-call | flops 1610612736 | bytes 7438336 | tf_op jit(solution)/shard_map/beside/pallas_call | solution.py:155
  20.6 0.2 convert.26
  20.8 0.1 slice_bitcast_fusion.3
  20.9 2.6 %collective-permute-start.6 = (f16[520,512]{1,0:T(8,128)(2,1)S(1)}, f16[520,512]{1,0:T(8,128)(2,1)S(1)}, u32[]{:S(2)}, u32[]{:S(2)}) collective-permute-start(f16[520,512]{1,0:T(8,128)(2,1)S(1)} %slice_bitcast_fusion.3), channel_id=1, source_target_pairs={{0,128},{128,0},{1,129},{129,1},{2,130},{130,2},{3,131},{131,3},{4... | collective-permute-start | bytes 1597448 | tf_op jit(solution)/shard_map/ppermute | solution.py:170
  23.5 0.3 convert.25
  23.7 0.2 slice_bitcast_fusion.4
  23.9 2.9 %collective-permute-start.8 = (f16[264,512]{1,0:T(8,128)(2,1)S(1)}, f16[264,512]{1,0:T(8,128)(2,1)S(1)}, u32[]{:S(2)}, u32[]{:S(2)}) collective-permute-start(f16[264,512]{1,0:T(8,128)(2,1)S(1)} %get-tuple-element.12), channel_id=1, source_target_pairs={{0,12},{4,0},{8,4},{12,8},{1,13},{5,1},{9,5},{13,9},{2,14},{6,2},{... | collective-permute-start | bytes 811016 | tf_op jit(solution)/shard_map/ppermute | solution.py:170
  26.8 4.7 %collective-permute-done.3 = f16[264,1024]{1,0:T(8,128)(2,1)S(1)} collective-permute-done((f16[264,1024]{1,0:T(8,128)(2,1)S(1)}, f16[264,1024]{1,0:T(8,128)(2,1)S(1)}, u32[]{:S(2)}, u32[]{:S(2)}) %collective-permute-start.3) | collective-permute-done | bytes 540704 | tf_op jit(solution)/shard_map/ppermute | solution.py:170
  31.5 4.7 %collective-permute-start.5 = (f16[264,512]{1,0:T(8,128)(2,1)S(1)}, f16[264,512]{1,0:T(8,128)(2,1)S(1)}, u32[]{:S(2)}, u32[]{:S(2)}) collective-permute-start(f16[264,512]{1,0:T(8,128)(2,1)S(1)} %get-tuple-element.14), channel_id=1, source_target_pairs={{0,4},{4,8},{8,12},{12,0},{1,5},{5,9},{9,13},{13,1},{2,6},{6,10},{... | collective-permute-start | bytes 811016 | tf_op jit(solution)/shard_map/ppermute | solution.py:170
  36.2 0.6 multiply_add_fusion
  36.8 0.7 first_x.1.refs_0_
  37.5 2.6 %collective-permute-start.4 = (f16[136,1024]{1,0:T(8,128)(2,1)S(1)}, f16[136,1024]{1,0:T(8,128)(2,1)S(1)}, u32[]{:S(2)}, u32[]{:S(2)}) collective-permute-start(f16[136,1024]{1,0:T(8,128)(2,1)S(1)} %fusion), channel_id=1, source_target_pairs={{0,128},{128,0},{1,129},{129,1},{2,130},{130,2},{3,131},{131,3},{4... | collective-permute-start | bytes 835592 | tf_op jit(solution)/shard_map/ppermute | solution.py:170
  40.1 0.1 convert_element_type.124.got_ref
  40.3 0.4 left_y.1.refs_4_
  40.6 0.1 convert.28
  40.9 2.2 %collective-permute-done.8 = f16[264,512]{1,0:T(8,128)(2,1)S(1)} collective-permute-done((f16[264,512]{1,0:T(8,128)(2,1)S(1)}, f16[264,512]{1,0:T(8,128)(2,1)S(1)}, u32[]{:S(2)}, u32[]{:S(2)}) %collective-permute-start.8) | collective-permute-done | bytes 270368 | tf_op jit(solution)/shard_map/ppermute | solution.py:170
  43.2 4.8 %collective-permute-start.10 = (f16[136,512]{1,0:T(8,128)(2,1)S(1)}, f16[136,512]{1,0:T(8,128)(2,1)S(1)}, u32[]{:S(2)}, u32[]{:S(2)}) collective-permute-start(f16[136,512]{1,0:T(8,128)(2,1)S(1)} %get-tuple-element.17), channel_id=1, source_target_pairs={{0,4},{4,8},{8,12},{12,0},{1,5},{5,9},{9,13},{13,1},{2,6},{6,10},{... | collective-permute-start | bytes 417800 | tf_op jit(solution)/shard_map/ppermute | solution.py:170
  48.1 0.4 right_x.1.refs_2_
  48.6 2.6 %collective-permute-start.9 = (f16[136,512]{1,0:T(8,128)(2,1)S(1)}, f16[136,512]{1,0:T(8,128)(2,1)S(1)}, u32[]{:S(2)}, u32[]{:S(2)}) collective-permute-start(f16[136,512]{1,0:T(8,128)(2,1)S(1)} %fusion.1), channel_id=1, source_target_pairs={{0,128},{128,0},{1,129},{129,1},{2,130},{130,2},{3,131},{131,3},{4... | collective-permute-start | bytes 417800 | tf_op jit(solution)/shard_map/ppermute | solution.py:170
  51.3 1.3 %collective-permute-done.10 = f16[136,512]{1,0:T(8,128)(2,1)S(1)} collective-permute-done((f16[136,512]{1,0:T(8,128)(2,1)S(1)}, f16[136,512]{1,0:T(8,128)(2,1)S(1)}, u32[]{:S(2)}, u32[]{:S(2)}) %collective-permute-start.10) | collective-permute-done | bytes 139296 | tf_op jit(solution)/shard_map/ppermute | solution.py:170
  52.6 2.6 %collective-permute-done.9 = f16[136,512]{1,0:T(8,128)(2,1)S(1)} collective-permute-done((f16[136,512]{1,0:T(8,128)(2,1)S(1)}, f16[136,512]{1,0:T(8,128)(2,1)S(1)}, u32[]{:S(2)}, u32[]{:S(2)}) %collective-permute-start.9) | collective-permute-done | bytes 139296 | tf_op jit(solution)/shard_map/ppermute | solution.py:170
  55.3 0.4 to_z.1
  55.7 24.9 %all_to_all.5 = f16[8,2,16,1152]{3,2,1,0:T(8,128)(2,1)S(1)} all-to-all(f16[8,2,16,1152]{3,2,1,0:T(8,128)(2,1)S(1)} %convert_element_type.138), channel_id=1, replica_groups=mesh['yh'=2,'z'=8,'x'=4,'yl'=2,'core'=2] {'z'}, dimensions={0} | all-to-all | bytes 1179648 | tf_op jit(solution)/shard_map/all_to_all | solution.py:213
  80.7 0.7 z_sum.1
  (29 shorter events, 0.8 us)
Async XLA Ops:
  0.0 18.3 %collective-permute-start.1 = (bf16[768,1024]{1,0:T(8,128)(2,1)}, bf16[768,1024]{1,0:T(8,128)(2,1)S(1)}, u32[]{:S(2)}, u32[]{:S(2)}) collective-permute-start(bf16[768,1024]{1,0:T(8,128)(2,1)} %own_ref.3), channel_id=1, source_target_pairs={{0,3},{1,0},{2,1},{3,2},{4,7},{5,4},{6,5},{7,6},{8,11},{9,8},{10,9... | collective-permute-start | bytes 4718600 | tf_op jit(solution)/shard_map/ppermute | solution.py:170
  0.0 1.4 %copy-start = (bf16[768,1024]{1,0:T(8,128)(2,1)S(1)}, bf16[768,1024]{1,0:T(8,128)(2,1)}, u32[]{:S(2)}) copy-start(bf16[768,1024]{1,0:T(8,128)(2,1)} %own_ref.3) | copy-start | bytes 4718596
  4.2 14.1 %copy-start.1 = (bf16[768,1024]{1,0:T(8,128)(2,1)S(1)}, bf16[768,1024]{1,0:T(8,128)(2,1)}, u32[]{:S(2)}) copy-start(bf16[768,1024]{1,0:T(8,128)(2,1)} %own_ref.3) | copy-start | bytes 4718596
  4.6 26.9 %collective-permute-start.3 = (f16[264,1024]{1,0:T(8,128)(2,1)S(1)}, f16[264,1024]{1,0:T(8,128)(2,1)S(1)}, u32[]{:S(2)}, u32[]{:S(2)}) collective-permute-start(f16[264,1024]{1,0:T(8,128)(2,1)S(1)} %get-tuple-element.9), channel_id=1, source_target_pairs={{0,12},{4,0},{8,4},{12,8},{1,13},{5,1},{9,5},{13,9},{2,14},{6,2},{... | collective-permute-start | bytes 1622024 | tf_op jit(solution)/shard_map/ppermute | solution.py:170
  7.4 24.0 %collective-permute-start.2 = (f16[264,1024]{1,0:T(8,128)(2,1)S(1)}, f16[264,1024]{1,0:T(8,128)(2,1)S(1)}, u32[]{:S(2)}, u32[]{:S(2)}) collective-permute-start(f16[264,1024]{1,0:T(8,128)(2,1)S(1)} %get-tuple-element.10), channel_id=1, source_target_pairs={{0,8},{4,12},{8,0},{12,4},{1,9},{5,13},{9,1},{13,5},{2,10},{6,14},... | collective-permute-start | bytes 1622024 | tf_op jit(solution)/shard_map/ppermute | solution.py:170
  8.3 27.9 %collective-permute-start = (f16[264,1024]{1,0:T(8,128)(2,1)S(1)}, f16[264,1024]{1,0:T(8,128)(2,1)S(1)}, u32[]{:S(2)}, u32[]{:S(2)}) collective-permute-start(f16[264,1024]{1,0:T(8,128)(2,1)S(1)} %get-tuple-element.11), channel_id=1, source_target_pairs={{0,4},{4,8},{8,12},{12,0},{1,5},{5,9},{9,13},{13,1},{2,6},{6,10},{... | collective-permute-start | bytes 1622024 | tf_op jit(solution)/shard_map/ppermute | solution.py:170
  20.9 19.2 %collective-permute-start.6 = (f16[520,512]{1,0:T(8,128)(2,1)S(1)}, f16[520,512]{1,0:T(8,128)(2,1)S(1)}, u32[]{:S(2)}, u32[]{:S(2)}) collective-permute-start(f16[520,512]{1,0:T(8,128)(2,1)S(1)} %slice_bitcast_fusion.3), channel_id=1, source_target_pairs={{0,128},{128,0},{1,129},{129,1},{2,130},{130,2},{3,131},{131,3},{4... | collective-permute-start | bytes 1597448 | tf_op jit(solution)/shard_map/ppermute | solution.py:170
  23.9 19.2 %collective-permute-start.8 = (f16[264,512]{1,0:T(8,128)(2,1)S(1)}, f16[264,512]{1,0:T(8,128)(2,1)S(1)}, u32[]{:S(2)}, u32[]{:S(2)}) collective-permute-start(f16[264,512]{1,0:T(8,128)(2,1)S(1)} %get-tuple-element.12), channel_id=1, source_target_pairs={{0,12},{4,0},{8,4},{12,8},{1,13},{5,1},{9,5},{13,9},{2,14},{6,2},{... | collective-permute-start | bytes 811016 | tf_op jit(solution)/shard_map/ppermute | solution.py:170
  31.5 11.7 %collective-permute-start.7 = (f16[264,512]{1,0:T(8,128)(2,1)S(1)}, f16[264,512]{1,0:T(8,128)(2,1)S(1)}, u32[]{:S(2)}, u32[]{:S(2)}) collective-permute-start(f16[264,512]{1,0:T(8,128)(2,1)S(1)} %get-tuple-element.13), channel_id=1, source_target_pairs={{0,8},{4,12},{8,0},{12,4},{1,9},{5,13},{9,1},{13,5},{2,10},{6,14},... | collective-permute-start | bytes 811016 | tf_op jit(solution)/shard_map/ppermute | solution.py:170
  31.5 16.6 %collective-permute-start.5 = (f16[264,512]{1,0:T(8,128)(2,1)S(1)}, f16[264,512]{1,0:T(8,128)(2,1)S(1)}, u32[]{:S(2)}, u32[]{:S(2)}) collective-permute-start(f16[264,512]{1,0:T(8,128)(2,1)S(1)} %get-tuple-element.14), channel_id=1, source_target_pairs={{0,4},{4,8},{8,12},{12,0},{1,5},{5,9},{9,13},{13,1},{2,6},{6,10},{... | collective-permute-start | bytes 811016 | tf_op jit(solution)/shard_map/ppermute | solution.py:170
  37.5 13.7 %collective-permute-start.4 = (f16[136,1024]{1,0:T(8,128)(2,1)S(1)}, f16[136,1024]{1,0:T(8,128)(2,1)S(1)}, u32[]{:S(2)}, u32[]{:S(2)}) collective-permute-start(f16[136,1024]{1,0:T(8,128)(2,1)S(1)} %fusion), channel_id=1, source_target_pairs={{0,128},{128,0},{1,129},{129,1},{2,130},{130,2},{3,131},{131,3},{4... | collective-permute-start | bytes 835592 | tf_op jit(solution)/shard_map/ppermute | solution.py:170
  40.8 10.4 %collective-permute-start.12 = (f16[136,512]{1,0:T(8,128)(2,1)S(1)}, f16[136,512]{1,0:T(8,128)(2,1)S(1)}, u32[]{:S(2)}, u32[]{:S(2)}) collective-permute-start(f16[136,512]{1,0:T(8,128)(2,1)S(1)} %get-tuple-element.15), channel_id=1, source_target_pairs={{0,12},{4,0},{8,4},{12,8},{1,13},{5,1},{9,5},{13,9},{2,14},{6,2},{... | collective-permute-start | bytes 417800 | tf_op jit(solution)/shard_map/ppermute | solution.py:170
  43.1 8.2 %collective-permute-start.11 = (f16[136,512]{1,0:T(8,128)(2,1)S(1)}, f16[136,512]{1,0:T(8,128)(2,1)S(1)}, u32[]{:S(2)}, u32[]{:S(2)}) collective-permute-start(f16[136,512]{1,0:T(8,128)(2,1)S(1)} %get-tuple-element.16), channel_id=1, source_target_pairs={{0,8},{4,12},{8,0},{12,4},{1,9},{5,13},{9,1},{13,5},{2,10},{6,14},... | collective-permute-start | bytes 417800 | tf_op jit(solution)/shard_map/ppermute | solution.py:170
  43.2 9.4 %collective-permute-start.10 = (f16[136,512]{1,0:T(8,128)(2,1)S(1)}, f16[136,512]{1,0:T(8,128)(2,1)S(1)}, u32[]{:S(2)}, u32[]{:S(2)}) collective-permute-start(f16[136,512]{1,0:T(8,128)(2,1)S(1)} %get-tuple-element.17), channel_id=1, source_target_pairs={{0,4},{4,8},{8,12},{12,0},{1,5},{5,9},{9,13},{13,1},{2,6},{6,10},{... | collective-permute-start | bytes 417800 | tf_op jit(solution)/shard_map/ppermute | solution.py:170
  48.6 6.6 %collective-permute-start.9 = (f16[136,512]{1,0:T(8,128)(2,1)S(1)}, f16[136,512]{1,0:T(8,128)(2,1)S(1)}, u32[]{:S(2)}, u32[]{:S(2)}) collective-permute-start(f16[136,512]{1,0:T(8,128)(2,1)S(1)} %fusion.1), channel_id=1, source_target_pairs={{0,128},{128,0},{1,129},{129,1},{2,130},{130,2},{3,131},{131,3},{4... | collective-permute-start | bytes 417800 | tf_op jit(solution)/shard_map/ppermute | solution.py:170

commit v4 on v3

--- a/solution.py
+++ b/solution.py
@@ -42,9 +42,10 @@
     return pl.ds(pl.multiple_of(start, 16), count)
 
 
-def senders(axis, blocks, growth):
+def senders(axis, blocks, growth, behind=None):
     powers = [jnp.max(block[block.shape[0] - 8 :, :128]) for block in blocks]
-    weights = [lowered(p, share(ahead(axis, -by), SIZES[axis])) for by, p in enumerate(powers)]
+    behind = behind or range(len(blocks))
+    weights = [lowered(p, share(ahead(axis, -by), SIZES[axis])) for by, p in zip(behind, powers)]
     return weights, functools.reduce(jnp.maximum, powers) + growth
 
 
@@ -78,7 +79,7 @@
     out_ref[:, out_ref.shape[1] - 8 :, :] = jnp.full((NX, 8, out_ref.shape[2]), power)
 
 
-def beside_kernel(own_ref, partner_ref, left_ref, right_ref):
+def beside_kernel(own_ref, partner_ref, _, left_ref, right_ref):
     half = left_ref.shape[2]
     by_y, by_x = share(lax.axis_index("yh"), NY), share(lax.axis_index("x"), NX)
 
@@ -94,10 +95,21 @@
     right_ref[:, right_ref.shape[1] - 8 :, :] = jnp.full((NX, 8, half), power)
 
 
-def x_to_y_kernel(own_ref, *refs):
+def relay_kernel(next_ref, before_ref, behind_ref, ahead_ref, out_ref):
+    count, half = out_ref.shape[1] - 8, out_ref.shape[2] // 2
+    (own, behind, beyond), power = senders("x", [next_ref.at[0], behind_ref, ahead_ref], 1.0, (0, 1, NX - 1))
+    up = lifted(power, share(lax.axis_index("x"), NX))
+    out_ref[0, :count, :half] = next_ref[0, :count, :half] * (own * up) + behind_ref[:count, :] * (behind * up)
+    out_ref[0, :count, half:] = next_ref[0, :count, half:] * (own * up)
+    out_ref[1, :count, :half] = before_ref[0, :count, :half] * (own * up)
+    out_ref[1, :count, half:] = before_ref[0, :count, half:] * (own * up) + ahead_ref[:count, :] * (beyond * up)
+    out_ref[:, count:, :] = jnp.full((2, 8, 2 * half), power)
+
+
+def x_to_y_kernel(behind, own_ref, *refs):
     out_ref = refs[-1]
     blocks = [own_ref.at[0], *refs[:-1]]
-    weights, power = senders("x", blocks, 2.0)
+    weights, power = senders("x", blocks, 2.0, behind)
     up = lifted(power, share(lax.axis_index("yh"), NY))
     count = out_ref.shape[1] - 8
     for by in range(NY):
@@ -125,31 +137,32 @@
     w_left, p_left = senders("x", left, 2.0)
     power = jnp.maximum(p_first, jnp.maximum(p_right, p_left))
     up = lifted(power, share(lax.axis_index("z"), NZ))
-    _, _, rows, wide = out_ref.shape
-    panel = wide - 128
+    _, rows, wide = out_ref.shape
+    panel = (wide - 128) // 2
     half = panel // 2
     for z in range(NZ):
         part = pl.ds(z * rows, rows)
         total = lambda blocks, weights: sum_of([block[part, :] * (w * up) for block, w in zip(blocks, weights)])
-        out_ref[z, 0, :, :panel] = total(first, w_first)
-        out_ref[z, 1, :, :half] = total(left, w_left)
-        out_ref[z, 1, :, half:panel] = total(right, w_right)
-    out_ref[:, :, :, panel:] = jnp.full((NZ, 2, rows, 128), power)
+        out_ref[z, :, :panel] = total(first, w_first)
+        out_ref[z, :, panel : panel + half] = total(left, w_left)
+        out_ref[z, :, panel + half : 2 * panel] = total(right, w_right)
+    out_ref[:, :, 2 * panel :] = jnp.full((NZ, rows, 128), power)
 
 
 def z_sum_kernel(scale, got_ref, out_ref):
     panel = out_ref.shape[2]
+    weights = [jnp.exp2(got_ref[s, :, 2 * panel :] - TOP) * (scale / float(1.0 - 0.5 * s / NZ)) for s in range(NZ)]
     for k in range(2):
-        weights = [jnp.exp2(got_ref[s, k, :, panel:] - TOP) * (scale / float(1.0 - 0.5 * s / NZ)) for s in range(NZ)]
         for j in range(panel // 128):
-            part = slice(j * 128, (j + 1) * 128)
-            out_ref[k, :, part] = sum_of([got_ref[s, k, :, part] * w for s, w in enumerate(weights)])
+            at = k * panel + j * 128
+            out_ref[k, :, j * 128 : (j + 1) * 128] = sum_of([got_ref[s, :, at : at + 128] * w for s, w in enumerate(weights)])
 
 
 def call(kernel, name, outs, *operands, flops=0):
-    whole = lambda shape: pl.BlockSpec(shape, lambda i: (0,) * len(shape))
+    block = lambda shape, n: pl.BlockSpec(shape, lambda i: (n,) + (0,) * (len(shape) - 1))
+    whole = lambda shape: block(shape, 0)
     arrays = [o[0] if isinstance(o, tuple) else o for o in operands]
-    specs = [whole((1, *o[0].shape[1:]) if isinstance(o, tuple) else o.shape) for o in operands]
+    specs = [block((1, *o[0].shape[1:]), o[1]) if isinstance(o, tuple) else whole(o.shape) for o in operands]
     out_shape = [jax.ShapeDtypeStruct(shape, jnp.float32) for shape in outs]
     moved = sum(a.size * a.dtype.itemsize for a in arrays) + sum(4 * s.size for s in out_shape)
     result = pl.pallas_call(
@@ -182,11 +195,14 @@
     partner = passed(acts, FACTOR, NF - 1)
 
     first = call(diagonal_kernel, "diagonal", [(NX, NY * NZ * rows + 8, panel)], acts, acts, flops=flops)
-    got_first = [passed(short(first[by]), "x", by) for by in range(1, NX)]
+    behind = long(passed(short(first[2, :, :half]), "x", 1))
+    beyond = long(passed(short(first[2, :, half:]), "x", NX - 1))
+    relay = call(relay_kernel, "relay", [(2, NY * NZ * rows + 8, panel)], (first, 1), (first, 3), behind, beyond)
+    got_first = [passed(short(relay[0]), "x", 1), passed(short(relay[1]), "x", NX - 1)]
 
     left, right = call(
         beside_kernel, "beside", [(NY, NX * NZ * rows + 8, half), (NX, NY * NZ * rows + 8, half)], acts, partner,
-        flops=flops,
+        (relay, 0), flops=flops,
     )
     left_sent, right_sent = short(left[1]), [short(right[by]) for by in range(1, NX)]
     got_left = passed(left_sent, "yh", 1)
@@ -196,18 +212,20 @@
     got_first = [long(g) + 0.0 * s for g, s in zip(got_first, ahead_of)]
 
     lines = NZ * rows + 8
-    first = call(x_to_y_kernel, "first_x", [(NY, lines, panel)], (first, 0), *got_first)
+    over_two = functools.partial(x_to_y_kernel, (0, 1, NX - 1))
+    over_all = functools.partial(x_to_y_kernel, None)
+    first = call(over_two, "first_x", [(NY, lines, panel)], (first, 0), *got_first)
     got_first = passed(short(first[1]), "yh", 1)
     left = call(y_to_x_kernel, "left_y", [(NX, lines, half)], (left, 0), long(got_left))
     left_sent = [short(left[by]) for by in range(1, NX)]
     got_left = [passed(s, "x", by) for by, s in enumerate(left_sent, 1)]
     ahead_of = [long(jnp.concatenate([s, s], axis=0)[: g.shape[0]]) for s, g in zip(left_sent, got_right)]
     got_right = [long(g) + 0.0 * s for g, s in zip(got_right, ahead_of)]
-    right = call(x_to_y_kernel, "right_x", [(NY, lines, half)], (right, 0), *got_right)
+    right = call(over_all, "right_x", [(NY, lines, half)], (right, 0), *got_right)
     got_right = passed(short(right[1]), "yh", 1)
 
     sent = call(
-        to_z_kernel, "to_z", [(NZ, 2, rows, panel + 128)],
+        to_z_kernel, "to_z", [(NZ, rows, 2 * panel + 128)],
         (first, 0), long(got_first), (right, 0), long(got_right), (left, 0), *map(long, got_left),
     )
     got = lax.all_to_all(short(sent), "z", 0, 0, tiled=True)

time: 82.3 us -> 79.4 us (0.965)
  starting transfers between devices: 24.7 us -> 15.3 us
  waiting for transfers between devices: 19.9 us -> 27.2 us
  blocking collectives: 24.9 us -> 23.6 us
    ppermute x13 -> x14, starting transfers between devices: 24.7 us -> 15.3 us  [passed(): lax.ppermute(value, axis, [(i, (i + by) % count) for i in range(count)])]
    ppermute x13 -> x14, waiting for transfers between devices: 19.9 us -> 27.2 us  [passed(): lax.ppermute(value, axis, [(i, (i + by) % count) for i in range(count)])]
    all_to_all x1, blocking collectives: 24.9 us -> 23.6 us  [per_device(): got = lax.all_to_all(short(sent), 'z', 0, 0, tiled=True)]
    pallas_call x7 -> x8, Pallas kernels: 7.17 us -> 7.46 us  [call(): pl.pallas_call(kernel, grid=(1,), out_shape=out_shape, in_specs=specs, ou...]
  transfers between devices with their start and end apart: 13 -> 14, of which waited for: 5 -> 8; matrix products, arithmetic and copies ran while one was open for 4% -> 4% of each run, Pallas kernels for 7% -> 8%
where the time goes in v4:
time: 79.4 us; the launch traced here: 78.5 us
  waiting for transfers between devices  27.2 us (34%)
  blocking collectives  23.6 us (30%)
  starting transfers between devices  15.3 us (19%)
  Pallas kernels  7.46 us (9%)
  other arithmetic  2.42 us (3%)
  local copies, waits for them, and re-layouts  2.21 us (3%)
    ppermute x14, waiting for transfers between devices, passed(): lax.ppermute(value, axis, [(i, (i + by) % count) for i in range(count)])  27.2 us
    all_to_all x1, blocking collectives, per_device(): got = lax.all_to_all(short(sent), 'z', 0, 0, tiled=True)  23.6 us
    ppermute x14, starting transfers between devices, passed(): lax.ppermute(value, axis, [(i, (i + by) % count) for i in range(count)])  15.3 us
    pallas_call x8, Pallas kernels, call(): pl.pallas_call(kernel, grid=(1,), out_shape=out_shape, in_specs=specs, ou...  7.46 us
  transfers between devices with their start and end apart: 14, of which 8 were waited for; matrix products, arithmetic and copies ran while one was open for 4% of the time, Pallas kernels for 8%

profile of v4, /device:TPU:8, one launch (start us, length us, event | category | flops | bytes accessed | tf_op | source)
XLA Modules:
  0.0 78.5 jit_solution(2585792170065489483)
XLA Ops:
  0.0 1.4 %copy-done = bf16[768,1024]{1,0:T(8,128)(2,1)S(1)} copy-done((bf16[768,1024]{1,0:T(8,128)(2,1)S(1)}, bf16[768,1024]{1,0:T(8,128)(2,1)}, u32[]{:S(2)}) %copy-start) | copy-done | bytes 1572888
  1.4 2.3 %diagonal.1.next_ref.before_ref.own_ref = f32[4,264,1024]{2,1,0:T(8,128)S(1)} custom-call(bf16[768,1024]{1,0:T(8,128)(2,1)S(1)} %copy-done, bf16[768,1024]{1,0:T(8,128)(2,1)S(1)} %copy-done), custom_call_target="tpu_custom_call" | custom-call | flops 1610612736 | bytes 7471104 | tf_op jit(solution)/shard_map/diagonal/pallas_call | solution.py:168
  3.7 0.4 convert.27
  4.3 2.8 %collective-permute-start.1 = (f16[264,512]{1,0:T(8,128)(2,1)S(1)}, f16[264,512]{1,0:T(8,128)(2,1)S(1)}, u32[]{:S(2)}, u32[]{:S(2)}) collective-permute-start(f16[264,512]{1,0:T(8,128)(2,1)S(1)} %get-tuple-element.9), channel_id=1, source_target_pairs={{0,12},{4,0},{8,4},{12,8},{1,13},{5,1},{9,5},{13,9},{2,14},{6,2},{... | collective-permute-start | bytes 811016 | tf_op jit(solution)/shard_map/ppermute | solution.py:183
  7.1 6.4 %collective-permute-done.1 = f16[264,512]{1,0:T(8,128)(2,1)S(1)} collective-permute-done((f16[264,512]{1,0:T(8,128)(2,1)S(1)}, f16[264,512]{1,0:T(8,128)(2,1)S(1)}, u32[]{:S(2)}, u32[]{:S(2)}) %collective-permute-start.1) | collective-permute-done | bytes 270368 | tf_op jit(solution)/shard_map/ppermute | solution.py:183
  13.6 3.3 %collective-permute-done = f16[264,512]{1,0:T(8,128)(2,1)S(1)} collective-permute-done((f16[264,512]{1,0:T(8,128)(2,1)S(1)}, f16[264,512]{1,0:T(8,128)(2,1)S(1)}, u32[]{:S(2)}, u32[]{:S(2)}) %collective-permute-start) | collective-permute-done | bytes 270368 | tf_op jit(solution)/shard_map/ppermute | solution.py:183
  17.0 0.5 relay.1._
  17.7 0.3 slice_bitcast_fusion
  17.9 0.4 collective-permute-start.4
  18.4 1.7 %collective-permute-start.2 = (f16[264,1024]{1,0:T(8,128)(2,1)S(1)}, f16[264,1024]{1,0:T(8,128)(2,1)S(1)}, u32[]{:S(2)}, u32[]{:S(2)}) collective-permute-start(f16[264,1024]{1,0:T(8,128)(2,1)S(1)} %get-tuple-element.15), channel_id=1, source_target_pairs={{0,4},{4,8},{8,12},{12,0},{1,5},{5,9},{9,13},{13,1},{2,6},{6,10},{... | collective-permute-start | bytes 1622024 | tf_op jit(solution)/shard_map/ppermute | solution.py:183
  20.0 2.3 %beside.1 = (f32[2,520,512]{2,1,0:T(8,128)S(1)}, f32[4,264,512]{2,1,0:T(8,128)S(1)}) custom-call(bf16[768,1024]{1,0:T(8,128)(2,1)S(1)} %copy-done.1, bf16[768,1024]{1,0:T(8,128)(2,1)S(1)} %collective-permute-done.3.partner_ref, f32[2,264,1024]{2,1,0:T(8,128)S(1)} %relay.1._), custom_call_target="tpu_custom_call" | custom-call | flops 1610612736 | bytes 9601024 | tf_op jit(solution)/shard_map/beside/pallas_call | solution.py:168
  22.3 0.2 convert.30
  22.7 2.4 %collective-permute-start.7 = (f16[520,512]{1,0:T(8,128)(2,1)S(1)}, f16[520,512]{1,0:T(8,128)(2,1)S(1)}, u32[]{:S(2)}, u32[]{:S(2)}) collective-permute-start(f16[520,512]{1,0:T(8,128)(2,1)S(1)} %slice_bitcast_fusion.2), channel_id=1, source_target_pairs={{0,128},{128,0},{1,129},{129,1},{2,130},{130,2},{3,131},{131,3},{4... | collective-permute-start | bytes 1597448 | tf_op jit(solution)/shard_map/ppermute | solution.py:183
  25.1 0.3 convert.29
  25.5 1.6 %collective-permute-start.9 = (f16[264,512]{1,0:T(8,128)(2,1)S(1)}, f16[264,512]{1,0:T(8,128)(2,1)S(1)}, u32[]{:S(2)}, u32[]{:S(2)}) collective-permute-start(f16[264,512]{1,0:T(8,128)(2,1)S(1)} %get-tuple-element.11), channel_id=1, source_target_pairs={{0,12},{4,0},{8,4},{12,8},{1,13},{5,1},{9,5},{13,9},{2,14},{6,2},{... | collective-permute-start | bytes 811016 | tf_op jit(solution)/shard_map/ppermute | solution.py:183
  27.2 0.5 collective-permute-start.8
  27.7 5.5 %collective-permute-done.4 = f16[264,1024]{1,0:T(8,128)(2,1)S(1)} collective-permute-done((f16[264,1024]{1,0:T(8,128)(2,1)S(1)}, f16[264,1024]{1,0:T(8,128)(2,1)S(1)}, u32[]{:S(2)}, u32[]{:S(2)}) %collective-permute-start.4) | collective-permute-done | bytes 540704 | tf_op jit(solution)/shard_map/ppermute | solution.py:183
  33.2 6.7 %collective-permute-done.2 = f16[264,1024]{1,0:T(8,128)(2,1)S(1)} collective-permute-done((f16[264,1024]{1,0:T(8,128)(2,1)S(1)}, f16[264,1024]{1,0:T(8,128)(2,1)S(1)}, u32[]{:S(2)}, u32[]{:S(2)}) %collective-permute-start.2) | collective-permute-done | bytes 540704 | tf_op jit(solution)/shard_map/ppermute | solution.py:183
  40.0 0.4 multiply_add_fusion
  40.3 0.5 first_x.1.refs_0_
  40.9 2.4 %collective-permute-start.5 = (f16[136,1024]{1,0:T(8,128)(2,1)S(1)}, f16[136,1024]{1,0:T(8,128)(2,1)S(1)}, u32[]{:S(2)}, u32[]{:S(2)}) collective-permute-start(f16[136,1024]{1,0:T(8,128)(2,1)S(1)} %fusion), channel_id=1, source_target_pairs={{0,128},{128,0},{1,129},{129,1},{2,130},{130,2},{3,131},{131,3},{4... | collective-permute-start | bytes 835592 | tf_op jit(solution)/shard_map/ppermute | solution.py:183
  43.4 0.4 left_y.1.refs_4_
  44.3 2.0 %collective-permute-start.11 = (f16[136,512]{1,0:T(8,128)(2,1)S(1)}, f16[136,512]{1,0:T(8,128)(2,1)S(1)}, u32[]{:S(2)}, u32[]{:S(2)}) collective-permute-start(f16[136,512]{1,0:T(8,128)(2,1)S(1)} %get-tuple-element.18), channel_id=1, source_target_pairs={{0,4},{4,8},{8,12},{12,0},{1,5},{5,9},{9,13},{13,1},{2,6},{6,10},{... | collective-permute-start | bytes 417800 | tf_op jit(solution)/shard_map/ppermute | solution.py:183
  46.5 0.4 right_x.1.refs_2_
  46.9 1.3 %collective-permute-start.10 = (f16[136,512]{1,0:T(8,128)(2,1)S(1)}, f16[136,512]{1,0:T(8,128)(2,1)S(1)}, u32[]{:S(2)}, u32[]{:S(2)}) collective-permute-start(f16[136,512]{1,0:T(8,128)(2,1)S(1)} %fusion.1), channel_id=1, source_target_pairs={{0,128},{128,0},{1,129},{129,1},{2,130},{130,2},{3,131},{131,3},{4... | collective-permute-start | bytes 417800 | tf_op jit(solution)/shard_map/ppermute | solution.py:183
  48.3 1.2 %collective-permute-done.5 = f16[136,1024]{1,0:T(8,128)(2,1)S(1)} collective-permute-done((f16[136,1024]{1,0:T(8,128)(2,1)S(1)}, f16[136,1024]{1,0:T(8,128)(2,1)S(1)}, u32[]{:S(2)}, u32[]{:S(2)}) %collective-permute-start.5) | collective-permute-done | bytes 278560 | tf_op jit(solution)/shard_map/ppermute | solution.py:183
  49.5 1.2 %collective-permute-done.12 = f16[136,512]{1,0:T(8,128)(2,1)S(1)} collective-permute-done((f16[136,512]{1,0:T(8,128)(2,1)S(1)}, f16[136,512]{1,0:T(8,128)(2,1)S(1)}, u32[]{:S(2)}, u32[]{:S(2)}) %collective-permute-start.12) | collective-permute-done | bytes 139296 | tf_op jit(solution)/shard_map/ppermute | solution.py:183
  50.8 1.4 %collective-permute-done.11 = f16[136,512]{1,0:T(8,128)(2,1)S(1)} collective-permute-done((f16[136,512]{1,0:T(8,128)(2,1)S(1)}, f16[136,512]{1,0:T(8,128)(2,1)S(1)}, u32[]{:S(2)}, u32[]{:S(2)}) %collective-permute-start.11) | collective-permute-done | bytes 139296 | tf_op jit(solution)/shard_map/ppermute | solution.py:183
  52.3 1.3 %collective-permute-done.10 = f16[136,512]{1,0:T(8,128)(2,1)S(1)} collective-permute-done((f16[136,512]{1,0:T(8,128)(2,1)S(1)}, f16[136,512]{1,0:T(8,128)(2,1)S(1)}, u32[]{:S(2)}, u32[]{:S(2)}) %collective-permute-start.10) | collective-permute-done | bytes 139296 | tf_op jit(solution)/shard_map/ppermute | solution.py:183
  53.6 0.4 to_z.1
  54.1 23.6 %all_to_all.5 = f16[8,16,2176]{2,1,0:T(8,128)(2,1)S(1)} all-to-all(f16[8,16,2176]{2,1,0:T(8,128)(2,1)S(1)} %convert_element_type.143), channel_id=1, replica_groups=mesh['yh'=2,'z'=8,'x'=4,'yl'=2,'core'=2] {'z'}, dimensions={0} | all-to-all | bytes 1114112 | tf_op jit(solution)/shard_map/all_to_all | solution.py:231
  77.8 0.7 z_sum.1
  (36 shorter events, 1.8 us)
Async XLA Ops:
  0.0 20.0 %collective-permute-start.3 = (bf16[768,1024]{1,0:T(8,128)(2,1)}, bf16[768,1024]{1,0:T(8,128)(2,1)S(1)}, u32[]{:S(2)}, u32[]{:S(2)}) collective-permute-start(bf16[768,1024]{1,0:T(8,128)(2,1)} %own_ref.3), channel_id=1, source_target_pairs={{0,3},{1,0},{2,1},{3,2},{4,7},{5,4},{6,5},{7,6},{8,11},{9,8},{10,9... | collective-permute-start | bytes 4718600 | tf_op jit(solution)/shard_map/ppermute | solution.py:183
  0.0 1.4 %copy-start = (bf16[768,1024]{1,0:T(8,128)(2,1)S(1)}, bf16[768,1024]{1,0:T(8,128)(2,1)}, u32[]{:S(2)}) copy-start(bf16[768,1024]{1,0:T(8,128)(2,1)} %own_ref.3) | copy-start | bytes 4718596
  4.3 9.2 %collective-permute-start.1 = (f16[264,512]{1,0:T(8,128)(2,1)S(1)}, f16[264,512]{1,0:T(8,128)(2,1)S(1)}, u32[]{:S(2)}, u32[]{:S(2)}) collective-permute-start(f16[264,512]{1,0:T(8,128)(2,1)S(1)} %get-tuple-element.9), channel_id=1, source_target_pairs={{0,12},{4,0},{8,4},{12,8},{1,13},{5,1},{9,5},{13,9},{2,14},{6,2},{... | collective-permute-start | bytes 811016 | tf_op jit(solution)/shard_map/ppermute | solution.py:183
  7.1 9.8 %collective-permute-start = (f16[264,512]{1,0:T(8,128)(2,1)S(1)}, f16[264,512]{1,0:T(8,128)(2,1)S(1)}, u32[]{:S(2)}, u32[]{:S(2)}) collective-permute-start(f16[264,512]{1,0:T(8,128)(2,1)S(1)} %get-tuple-element.10), channel_id=1, source_target_pairs={{0,4},{4,8},{8,12},{12,0},{1,5},{5,9},{9,13},{13,1},{2,6},{6,10},{... | collective-permute-start | bytes 811016 | tf_op jit(solution)/shard_map/ppermute | solution.py:183
  17.6 2.4 %copy-start.1 = (bf16[768,1024]{1,0:T(8,128)(2,1)S(1)}, bf16[768,1024]{1,0:T(8,128)(2,1)}, u32[]{:S(2)}) copy-start(bf16[768,1024]{1,0:T(8,128)(2,1)} %own_ref.3) | copy-start | bytes 4718596
  17.9 15.3 %collective-permute-start.4 = (f16[264,1024]{1,0:T(8,128)(2,1)S(1)}, f16[264,1024]{1,0:T(8,128)(2,1)S(1)}, u32[]{:S(2)}, u32[]{:S(2)}) collective-permute-start(f16[264,1024]{1,0:T(8,128)(2,1)S(1)} %get-tuple-element.14), channel_id=1, source_target_pairs={{0,12},{4,0},{8,4},{12,8},{1,13},{5,1},{9,5},{13,9},{2,14},{6,2},{... | collective-permute-start | bytes 1622024 | tf_op jit(solution)/shard_map/ppermute | solution.py:183
  18.4 21.6 %collective-permute-start.2 = (f16[264,1024]{1,0:T(8,128)(2,1)S(1)}, f16[264,1024]{1,0:T(8,128)(2,1)S(1)}, u32[]{:S(2)}, u32[]{:S(2)}) collective-permute-start(f16[264,1024]{1,0:T(8,128)(2,1)S(1)} %get-tuple-element.15), channel_id=1, source_target_pairs={{0,4},{4,8},{8,12},{12,0},{1,5},{5,9},{9,13},{13,1},{2,6},{6,10},{... | collective-permute-start | bytes 1622024 | tf_op jit(solution)/shard_map/ppermute | solution.py:183
  22.7 20.6 %collective-permute-start.7 = (f16[520,512]{1,0:T(8,128)(2,1)S(1)}, f16[520,512]{1,0:T(8,128)(2,1)S(1)}, u32[]{:S(2)}, u32[]{:S(2)}) collective-permute-start(f16[520,512]{1,0:T(8,128)(2,1)S(1)} %slice_bitcast_fusion.2), channel_id=1, source_target_pairs={{0,128},{128,0},{1,129},{129,1},{2,130},{130,2},{3,131},{131,3},{4... | collective-permute-start | bytes 1597448 | tf_op jit(solution)/shard_map/ppermute | solution.py:183
  25.5 18.6 %collective-permute-start.9 = (f16[264,512]{1,0:T(8,128)(2,1)S(1)}, f16[264,512]{1,0:T(8,128)(2,1)S(1)}, u32[]{:S(2)}, u32[]{:S(2)}) collective-permute-start(f16[264,512]{1,0:T(8,128)(2,1)S(1)} %get-tuple-element.11), channel_id=1, source_target_pairs={{0,12},{4,0},{8,4},{12,8},{1,13},{5,1},{9,5},{13,9},{2,14},{6,2},{... | collective-permute-start | bytes 811016 | tf_op jit(solution)/shard_map/ppermute | solution.py:183
  27.2 17.1 %collective-permute-start.8 = (f16[264,512]{1,0:T(8,128)(2,1)S(1)}, f16[264,512]{1,0:T(8,128)(2,1)S(1)}, u32[]{:S(2)}, u32[]{:S(2)}) collective-permute-start(f16[264,512]{1,0:T(8,128)(2,1)S(1)} %get-tuple-element.12), channel_id=1, source_target_pairs={{0,8},{4,12},{8,0},{12,4},{1,9},{5,13},{9,1},{13,5},{2,10},{6,14},... | collective-permute-start | bytes 811016 | tf_op jit(solution)/shard_map/ppermute | solution.py:183
  33.2 13.2 %collective-permute-start.6 = (f16[264,512]{1,0:T(8,128)(2,1)S(1)}, f16[264,512]{1,0:T(8,128)(2,1)S(1)}, u32[]{:S(2)}, u32[]{:S(2)}) collective-permute-start(f16[264,512]{1,0:T(8,128)(2,1)S(1)} %get-tuple-element.13), channel_id=1, source_target_pairs={{0,4},{4,8},{8,12},{12,0},{1,5},{5,9},{9,13},{13,1},{2,6},{6,10},{... | collective-permute-start | bytes 811016 | tf_op jit(solution)/shard_map/ppermute | solution.py:183
  40.9 8.5 %collective-permute-start.5 = (f16[136,1024]{1,0:T(8,128)(2,1)S(1)}, f16[136,1024]{1,0:T(8,128)(2,1)S(1)}, u32[]{:S(2)}, u32[]{:S(2)}) collective-permute-start(f16[136,1024]{1,0:T(8,128)(2,1)S(1)} %fusion), channel_id=1, source_target_pairs={{0,128},{128,0},{1,129},{129,1},{2,130},{130,2},{3,131},{131,3},{4... | collective-permute-start | bytes 835592 | tf_op jit(solution)/shard_map/ppermute | solution.py:183
  44.0 5.5 %collective-permute-start.13 = (f16[136,512]{1,0:T(8,128)(2,1)S(1)}, f16[136,512]{1,0:T(8,128)(2,1)S(1)}, u32[]{:S(2)}, u32[]{:S(2)}) collective-permute-start(f16[136,512]{1,0:T(8,128)(2,1)S(1)} %get-tuple-element.16), channel_id=1, source_target_pairs={{0,12},{4,0},{8,4},{12,8},{1,13},{5,1},{9,5},{13,9},{2,14},{6,2},{... | collective-permute-start | bytes 417800 | tf_op jit(solution)/shard_map/ppermute | solution.py:183
  44.1 6.7 %collective-permute-start.12 = (f16[136,512]{1,0:T(8,128)(2,1)S(1)}, f16[136,512]{1,0:T(8,128)(2,1)S(1)}, u32[]{:S(2)}, u32[]{:S(2)}) collective-permute-start(f16[136,512]{1,0:T(8,128)(2,1)S(1)} %get-tuple-element.17), channel_id=1, source_target_pairs={{0,8},{4,12},{8,0},{12,4},{1,9},{5,13},{9,1},{13,5},{2,10},{6,14},... | collective-permute-start | bytes 417800 | tf_op jit(solution)/shard_map/ppermute | solution.py:183
  44.3 7.9 %collective-permute-start.11 = (f16[136,512]{1,0:T(8,128)(2,1)S(1)}, f16[136,512]{1,0:T(8,128)(2,1)S(1)}, u32[]{:S(2)}, u32[]{:S(2)}) collective-permute-start(f16[136,512]{1,0:T(8,128)(2,1)S(1)} %get-tuple-element.18), channel_id=1, source_target_pairs={{0,4},{4,8},{8,12},{12,0},{1,5},{5,9},{9,13},{13,1},{2,6},{6,10},{... | collective-permute-start | bytes 417800 | tf_op jit(solution)/shard_map/ppermute | solution.py:183
  46.9 6.6 %collective-permute-start.10 = (f16[136,512]{1,0:T(8,128)(2,1)S(1)}, f16[136,512]{1,0:T(8,128)(2,1)S(1)}, u32[]{:S(2)}, u32[]{:S(2)}) collective-permute-start(f16[136,512]{1,0:T(8,128)(2,1)S(1)} %fusion.1), channel_id=1, source_target_pairs={{0,128},{128,0},{1,129},{129,1},{2,130},{130,2},{3,131},{131,3},{4... | collective-permute-start | bytes 417800 | tf_op jit(solution)/shard_map/ppermute | solution.py:183

commit v5 on v4

--- a/solution.py
+++ b/solution.py
@@ -88,7 +88,10 @@
         to_x = lax.rem(x - lax.axis_index("x") + NX, NX)
         to_y = lax.rem(y - lax.axis_index("yh") + NY, NY)
         left_ref[to_y, rows_of((to_x * NZ + z) * rows, rows), :] = value[:, :half] * by_y
-        right_ref[to_x, rows_of((y * NZ + z) * rows, rows), :] = value[:, half:] * by_x
+        part, middle = rows_of((y * NZ + z) * rows, rows), right_ref.shape[2] // 2
+        slot = jnp.where(to_x == 0, 0, lax.rem(to_x + 1, NX - 1) + 1)
+        right_ref[slot, part, :middle] = value[:, half : half + middle] * by_x
+        right_ref[to_x, part, middle:] = value[:, half + middle :] * by_x
 
     power = products(own_ref, partner_ref, visit)
     left_ref[:, left_ref.shape[1] - 8 :, :] = jnp.full((NY, 8, half), power)
@@ -104,6 +107,32 @@
     out_ref[1, :count, :half] = before_ref[0, :count, :half] * (own * up)
     out_ref[1, :count, half:] = before_ref[0, :count, half:] * (own * up) + ahead_ref[:count, :] * (beyond * up)
     out_ref[:, count:, :] = jnp.full((2, 8, 2 * half), power)
+
+
+def join_kernel(joins_ref, behind_ref, ahead_ref, out_ref):
+    count, half = out_ref.shape[1] - 8, out_ref.shape[2]
+    (own, behind, beyond), power = senders("x", [joins_ref.at[0], behind_ref, ahead_ref], 1.0, (0, 1, NX - 1))
+    up = lifted(power, share(lax.axis_index("x"), NX))
+    out_ref[0, :count, :] = joins_ref[0, :count, :half] * (own * up) + behind_ref[:count, :half] * (behind * up)
+    out_ref[1, :count, :] = joins_ref[0, :count, half:] * (own * up) + ahead_ref[:count, half:] * (beyond * up)
+    out_ref[:, count:, :] = jnp.full((2, 8, half), power)
+
+
+def joined_to_y_kernel(own_ref, behind_ref, ahead_ref, from_behind_ref, from_ahead_ref, out_ref):
+    count, half = out_ref.shape[1] - 8, out_ref.shape[2] // 2
+    blocks = [own_ref.at[0], behind_ref, ahead_ref, from_behind_ref, from_ahead_ref]
+    weights, power = senders("x", blocks, 2.0, (0, 1, NX - 1, 1, NX - 1))
+    up = lifted(power, share(lax.axis_index("yh"), NY))
+    own, behind, beyond, from_behind, from_ahead = (w * up for w in weights)
+    for by in range(NY):
+        part = rows_of(ahead("yh", by) * count, count)
+        out_ref[by, :count, :half] = (
+            own_ref[0, part, :half] * own + ahead_ref[part, :half] * beyond + from_behind_ref[part, :] * from_behind
+        )
+        out_ref[by, :count, half:] = (
+            own_ref[0, part, half:] * own + behind_ref[part, half:] * behind + from_ahead_ref[part, :] * from_ahead
+        )
+    out_ref[:, count:, :] = jnp.full((NY, 8, 2 * half), power)
 
 
 def x_to_y_kernel(behind, own_ref, *refs):
@@ -204,24 +233,26 @@
         beside_kernel, "beside", [(NY, NX * NZ * rows + 8, half), (NX, NY * NZ * rows + 8, half)], acts, partner,
         (relay, 0), flops=flops,
     )
-    left_sent, right_sent = short(left[1]), [short(right[by]) for by in range(1, NX)]
+    quarter = half // 2
+    left_sent, right_sent = short(left[1]), [short(right[1]), short(right[2])]
     got_left = passed(left_sent, "yh", 1)
-    got_right = [passed(right_sent[by - 1], "x", by) for by in range(1, NX)]
-
-    ahead_of = [long(jnp.concatenate([s, left_sent[: s.shape[0]]], axis=1)) for s in right_sent]
-    got_first = [long(g) + 0.0 * s for g, s in zip(got_first, ahead_of)]
+    behind, beyond = long(passed(right_sent[0], "x", 1)), long(passed(right_sent[1], "x", NX - 1))
+
+    ahead_of = long(jnp.concatenate([right_sent[1], left_sent[: right_sent[1].shape[0]]], axis=1))
+    got_first = [long(g) + 0.0 * ahead_of for g in got_first]
+    relay = call(join_kernel, "join", [(2, NY * NZ * rows + 8, quarter)], (right, 3), behind, beyond)
+    got_right = [passed(short(relay[0]), "x", 1), passed(short(relay[1]), "x", NX - 1)]
 
     lines = NZ * rows + 8
     over_two = functools.partial(x_to_y_kernel, (0, 1, NX - 1))
-    over_all = functools.partial(x_to_y_kernel, None)
     first = call(over_two, "first_x", [(NY, lines, panel)], (first, 0), *got_first)
     got_first = passed(short(first[1]), "yh", 1)
     left = call(y_to_x_kernel, "left_y", [(NX, lines, half)], (left, 0), long(got_left))
     left_sent = [short(left[by]) for by in range(1, NX)]
     got_left = [passed(s, "x", by) for by, s in enumerate(left_sent, 1)]
-    ahead_of = [long(jnp.concatenate([s, s], axis=0)[: g.shape[0]]) for s, g in zip(left_sent, got_right)]
-    got_right = [long(g) + 0.0 * s for g, s in zip(got_right, ahead_of)]
-    right = call(over_all, "right_x", [(NY, lines, half)], (right, 0), *got_right)
+    tied = [long(jnp.concatenate([s, s], axis=0)[: g.shape[0], :quarter]) for s, g in zip(left_sent, got_right)]
+    got_right = [long(g) + 0.0 * s for g, s in zip(got_right, tied)]
+    right = call(joined_to_y_kernel, "right_x", [(NY, lines, half)], (right, 0), behind, beyond, *got_right)
     got_right = passed(short(right[1]), "yh", 1)
 
     sent = call(

time: 79.4 us -> 78.4 us (0.987)
  waiting for transfers between devices: 27.2 us -> 20.9 us
  starting transfers between devices: 15.3 us -> 21.2 us
    ppermute x14 -> x15, waiting for transfers between devices: 27.2 us -> 20.9 us  [passed(): lax.ppermute(value, axis, [(i, (i + by) % count) for i in range(count)])]
    ppermute x14 -> x15, starting transfers between devices: 15.3 us -> 21.2 us  [passed(): lax.ppermute(value, axis, [(i, (i + by) % count) for i in range(count)])]
    pallas_call x8 -> x9, Pallas kernels: 7.46 us -> 7.66 us  [call(): pl.pallas_call(kernel, grid=(1,), out_shape=out_shape, in_specs=specs, ou...]
  transfers between devices with their start and end apart: 14 -> 15, of which waited for: 8 -> 9; matrix products, arithmetic and copies ran while one was open for 4% -> 4% of each run, Pallas kernels for 8% -> 8%
where the time goes in v5:
time: 78.4 us; the launch traced here: 77.8 us
  blocking collectives  23.2 us (30%)
  starting transfers between devices  21.2 us (27%)
  waiting for transfers between devices  20.9 us (27%)
  Pallas kernels  7.66 us (10%)
  other arithmetic  2.37 us (3%)
  local copies, waits for them, and re-layouts  2.2 us (3%)
    all_to_all x1, blocking collectives, per_device(): got = lax.all_to_all(short(sent), 'z', 0, 0, tiled=True)  23.2 us
    ppermute x15, starting transfers between devices, passed(): lax.ppermute(value, axis, [(i, (i + by) % count) for i in range(count)])  21.2 us
    ppermute x15, waiting for transfers between devices, passed(): lax.ppermute(value, axis, [(i, (i + by) % count) for i in range(count)])  20.9 us
    pallas_call x9, Pallas kernels, call(): pl.pallas_call(kernel, grid=(1,), out_shape=out_shape, in_specs=specs, ou...  7.66 us
  transfers between devices with their start and end apart: 15, of which 9 were waited for; matrix products, arithmetic and copies ran while one was open for 4% of the time, Pallas kernels for 8%

profile of v5, /device:TPU:8, one launch (start us, length us, event | category | flops | bytes accessed | tf_op | source)
XLA Modules:
  0.0 77.8 jit_solution(4331887519700849824)
XLA Ops:
  0.0 1.4 %copy-done = bf16[768,1024]{1,0:T(8,128)(2,1)S(1)} copy-done((bf16[768,1024]{1,0:T(8,128)(2,1)S(1)}, bf16[768,1024]{1,0:T(8,128)(2,1)}, u32[]{:S(2)}) %copy-start) | copy-done | bytes 1572888
  1.4 2.3 %diagonal.1.next_ref.before_ref.own_ref = f32[4,264,1024]{2,1,0:T(8,128)S(1)} custom-call(bf16[768,1024]{1,0:T(8,128)(2,1)S(1)} %copy-done, bf16[768,1024]{1,0:T(8,128)(2,1)S(1)} %copy-done), custom_call_target="tpu_custom_call" | custom-call | flops 1610612736 | bytes 7471104 | tf_op jit(solution)/shard_map/diagonal/pallas_call | solution.py:197
  3.7 0.4 convert.30
  4.3 2.8 %collective-permute-start.1 = (f16[264,512]{1,0:T(8,128)(2,1)S(1)}, f16[264,512]{1,0:T(8,128)(2,1)S(1)}, u32[]{:S(2)}, u32[]{:S(2)}) collective-permute-start(f16[264,512]{1,0:T(8,128)(2,1)S(1)} %get-tuple-element.9), channel_id=1, source_target_pairs={{0,12},{4,0},{8,4},{12,8},{1,13},{5,1},{9,5},{13,9},{2,14},{6,2},{... | collective-permute-start | bytes 811016 | tf_op jit(solution)/shard_map/ppermute | solution.py:212
  7.1 6.4 %collective-permute-done.1 = f16[264,512]{1,0:T(8,128)(2,1)S(1)} collective-permute-done((f16[264,512]{1,0:T(8,128)(2,1)S(1)}, f16[264,512]{1,0:T(8,128)(2,1)S(1)}, u32[]{:S(2)}, u32[]{:S(2)}) %collective-permute-start.1) | collective-permute-done | bytes 270368 | tf_op jit(solution)/shard_map/ppermute | solution.py:212
  13.6 3.3 %collective-permute-done = f16[264,512]{1,0:T(8,128)(2,1)S(1)} collective-permute-done((f16[264,512]{1,0:T(8,128)(2,1)S(1)}, f16[264,512]{1,0:T(8,128)(2,1)S(1)}, u32[]{:S(2)}, u32[]{:S(2)}) %collective-permute-start) | collective-permute-done | bytes 270368 | tf_op jit(solution)/shard_map/ppermute | solution.py:212
  17.0 0.4 relay.1._
  17.6 0.3 slice_bitcast_fusion
  17.9 0.4 collective-permute-start.4
  18.4 1.7 %collective-permute-start.2 = (f16[264,1024]{1,0:T(8,128)(2,1)S(1)}, f16[264,1024]{1,0:T(8,128)(2,1)S(1)}, u32[]{:S(2)}, u32[]{:S(2)}) collective-permute-start(f16[264,1024]{1,0:T(8,128)(2,1)S(1)} %get-tuple-element.14), channel_id=1, source_target_pairs={{0,4},{4,8},{8,12},{12,0},{1,5},{5,9},{9,13},{13,1},{2,6},{6,10},{... | collective-permute-start | bytes 1622024 | tf_op jit(solution)/shard_map/ppermute | solution.py:212
  20.0 2.3 %beside.1 = (f32[2,520,512]{2,1,0:T(8,128)S(1)}, f32[4,264,512]{2,1,0:T(8,128)S(1)}) custom-call(bf16[768,1024]{1,0:T(8,128)(2,1)S(1)} %copy-done.1, bf16[768,1024]{1,0:T(8,128)(2,1)S(1)} %collective-permute-done.3.partner_ref, f32[2,264,1024]{2,1,0:T(8,128)S(1)} %relay.1._), custom_call_target="tpu_custom_call" | custom-call | flops 1610612736 | bytes 9601024 | tf_op jit(solution)/shard_map/beside/pallas_call | solution.py:197
  22.7 2.4 %collective-permute-start.9 = (f16[520,512]{1,0:T(8,128)(2,1)S(1)}, f16[520,512]{1,0:T(8,128)(2,1)S(1)}, u32[]{:S(2)}, u32[]{:S(2)}) collective-permute-start(f16[520,512]{1,0:T(8,128)(2,1)S(1)} %slice_bitcast_fusion.2), channel_id=1, source_target_pairs={{0,128},{128,0},{1,129},{129,1},{2,130},{130,2},{3,131},{131,3},{4... | collective-permute-start | bytes 1597448 | tf_op jit(solution)/shard_map/ppermute | solution.py:212
  25.6 3.2 %collective-permute-start.7 = (f16[264,512]{1,0:T(8,128)(2,1)S(1)}, f16[264,512]{1,0:T(8,128)(2,1)S(1)}, u32[]{:S(2)}, u32[]{:S(2)}) collective-permute-start(f16[264,512]{1,0:T(8,128)(2,1)S(1)} %get-tuple-element.12), channel_id=1, source_target_pairs={{0,12},{4,0},{8,4},{12,8},{1,13},{5,1},{9,5},{13,9},{2,14},{6,2},{... | collective-permute-start | bytes 811016 | tf_op jit(solution)/shard_map/ppermute | solution.py:212
  28.8 4.4 %collective-permute-done.4 = f16[264,1024]{1,0:T(8,128)(2,1)S(1)} collective-permute-done((f16[264,1024]{1,0:T(8,128)(2,1)S(1)}, f16[264,1024]{1,0:T(8,128)(2,1)S(1)}, u32[]{:S(2)}, u32[]{:S(2)}) %collective-permute-start.4) | collective-permute-done | bytes 540704 | tf_op jit(solution)/shard_map/ppermute | solution.py:212
  33.2 1.6 %collective-permute-done.2 = f16[264,1024]{1,0:T(8,128)(2,1)S(1)} collective-permute-done((f16[264,1024]{1,0:T(8,128)(2,1)S(1)}, f16[264,1024]{1,0:T(8,128)(2,1)S(1)}, u32[]{:S(2)}, u32[]{:S(2)}) %collective-permute-start.2) | collective-permute-done | bytes 540704 | tf_op jit(solution)/shard_map/ppermute | solution.py:212
  34.8 0.4 convert_add_fusion
  35.2 0.5 first_x.1.refs_0_
  35.7 2.4 %collective-permute-start.5 = (f16[136,1024]{1,0:T(8,128)(2,1)S(1)}, f16[136,1024]{1,0:T(8,128)(2,1)S(1)}, u32[]{:S(2)}, u32[]{:S(2)}) collective-permute-start(f16[136,1024]{1,0:T(8,128)(2,1)S(1)} %fusion.1), channel_id=1, source_target_pairs={{0,128},{128,0},{1,129},{129,1},{2,130},{130,2},{3,131},{131,3},{4... | collective-permute-start | bytes 835592 | tf_op jit(solution)/shard_map/ppermute | solution.py:212
  38.1 0.9 %collective-permute-done.6 = f16[264,512]{1,0:T(8,128)(2,1)S(1)} collective-permute-done((f16[264,512]{1,0:T(8,128)(2,1)S(1)}, f16[264,512]{1,0:T(8,128)(2,1)S(1)}, u32[]{:S(2)}, u32[]{:S(2)}) %collective-permute-start.6) | collective-permute-done | bytes 270368 | tf_op jit(solution)/shard_map/ppermute | solution.py:212
  39.5 0.3 collective-permute-start.10
  39.8 1.8 %collective-permute-start.8 = (f16[264,256]{1,0:T(8,128)(2,1)S(1)}, f16[264,256]{1,0:T(8,128)(2,1)S(1)}, u32[]{:S(2)}, u32[]{:S(2)}) collective-permute-start(f16[264,256]{1,0:T(8,128)(2,1)S(1)} %get-tuple-element.21), channel_id=1, source_target_pairs={{0,4},{4,8},{8,12},{12,0},{1,5},{5,9},{9,13},{13,1},{2,6},{6,10},{... | collective-permute-start | bytes 405512 | tf_op jit(solution)/shard_map/ppermute | solution.py:212
  41.7 0.4 left_y.1.refs_4_
  42.3 1.5 %collective-permute-start.14 = (f16[136,512]{1,0:T(8,128)(2,1)S(1)}, f16[136,512]{1,0:T(8,128)(2,1)S(1)}, u32[]{:S(2)}, u32[]{:S(2)}) collective-permute-start(f16[136,512]{1,0:T(8,128)(2,1)S(1)} %get-tuple-element.15), channel_id=1, source_target_pairs={{0,12},{4,0},{8,4},{12,8},{1,13},{5,1},{9,5},{13,9},{2,14},{6,2},{... | collective-permute-start | bytes 417800 | tf_op jit(solution)/shard_map/ppermute | solution.py:212
  43.8 0.8 %collective-permute-start.13 = (f16[136,512]{1,0:T(8,128)(2,1)S(1)}, f16[136,512]{1,0:T(8,128)(2,1)S(1)}, u32[]{:S(2)}, u32[]{:S(2)}) collective-permute-start(f16[136,512]{1,0:T(8,128)(2,1)S(1)} %get-tuple-element.16), channel_id=1, source_target_pairs={{0,8},{4,12},{8,0},{12,4},{1,9},{5,13},{9,1},{13,5},{2,10},{6,14},... | collective-permute-start | bytes 417800 | tf_op jit(solution)/shard_map/ppermute | solution.py:212
  44.6 1.5 %collective-permute-done.10 = f16[264,256]{1,0:T(8,128)(2,1)S(1)} collective-permute-done((f16[264,256]{1,0:T(8,128)(2,1)S(1)}, f16[264,256]{1,0:T(8,128)(2,1)S(1)}, u32[]{:S(2)}, u32[]{:S(2)}) %collective-permute-start.10) | collective-permute-done | bytes 135200 | tf_op jit(solution)/shard_map/ppermute | solution.py:212
  46.2 0.3 right_x.1.refs_2_
  46.6 3.7 %collective-permute-start.11 = (f16[136,512]{1,0:T(8,128)(2,1)S(1)}, f16[136,512]{1,0:T(8,128)(2,1)S(1)}, u32[]{:S(2)}, u32[]{:S(2)}) collective-permute-start(f16[136,512]{1,0:T(8,128)(2,1)S(1)} %fusion.2), channel_id=1, source_target_pairs={{0,128},{128,0},{1,129},{129,1},{2,130},{130,2},{3,131},{131,3},{4... | collective-permute-start | bytes 417800 | tf_op jit(solution)/shard_map/ppermute | solution.py:212
  50.5 1.8 %collective-permute-done.12 = f16[136,512]{1,0:T(8,128)(2,1)S(1)} collective-permute-done((f16[136,512]{1,0:T(8,128)(2,1)S(1)}, f16[136,512]{1,0:T(8,128)(2,1)S(1)}, u32[]{:S(2)}, u32[]{:S(2)}) %collective-permute-start.12) | collective-permute-done | bytes 139296 | tf_op jit(solution)/shard_map/ppermute | solution.py:212
  52.3 1.0 %collective-permute-done.11 = f16[136,512]{1,0:T(8,128)(2,1)S(1)} collective-permute-done((f16[136,512]{1,0:T(8,128)(2,1)S(1)}, f16[136,512]{1,0:T(8,128)(2,1)S(1)}, u32[]{:S(2)}, u32[]{:S(2)}) %collective-permute-start.11) | collective-permute-done | bytes 139296 | tf_op jit(solution)/shard_map/ppermute | solution.py:212
  53.3 0.4 to_z.1
  53.8 23.2 %all_to_all.5 = f16[8,16,2176]{2,1,0:T(8,128)(2,1)S(1)} all-to-all(f16[8,16,2176]{2,1,0:T(8,128)(2,1)S(1)} %convert_element_type.144), channel_id=1, replica_groups=mesh['yh'=2,'z'=8,'x'=4,'yl'=2,'core'=2] {'z'}, dimensions={0} | all-to-all | bytes 1114112 | tf_op jit(solution)/shard_map/all_to_all | solution.py:262
  77.1 0.7 z_sum.1
  (42 shorter events, 2.7 us)
Async XLA Ops:
  0.0 20.0 %collective-permute-start.3 = (bf16[768,1024]{1,0:T(8,128)(2,1)}, bf16[768,1024]{1,0:T(8,128)(2,1)S(1)}, u32[]{:S(2)}, u32[]{:S(2)}) collective-permute-start(bf16[768,1024]{1,0:T(8,128)(2,1)} %own_ref.3), channel_id=1, source_target_pairs={{0,3},{1,0},{2,1},{3,2},{4,7},{5,4},{6,5},{7,6},{8,11},{9,8},{10,9... | collective-permute-start | bytes 4718600 | tf_op jit(solution)/shard_map/ppermute | solution.py:212
  0.0 1.4 %copy-start = (bf16[768,1024]{1,0:T(8,128)(2,1)S(1)}, bf16[768,1024]{1,0:T(8,128)(2,1)}, u32[]{:S(2)}) copy-start(bf16[768,1024]{1,0:T(8,128)(2,1)} %own_ref.3) | copy-start | bytes 4718596
  4.3 9.2 %collective-permute-start.1 = (f16[264,512]{1,0:T(8,128)(2,1)S(1)}, f16[264,512]{1,0:T(8,128)(2,1)S(1)}, u32[]{:S(2)}, u32[]{:S(2)}) collective-permute-start(f16[264,512]{1,0:T(8,128)(2,1)S(1)} %get-tuple-element.9), channel_id=1, source_target_pairs={{0,12},{4,0},{8,4},{12,8},{1,13},{5,1},{9,5},{13,9},{2,14},{6,2},{... | collective-permute-start | bytes 811016 | tf_op jit(solution)/shard_map/ppermute | solution.py:212
  7.1 9.8 %collective-permute-start = (f16[264,512]{1,0:T(8,128)(2,1)S(1)}, f16[264,512]{1,0:T(8,128)(2,1)S(1)}, u32[]{:S(2)}, u32[]{:S(2)}) collective-permute-start(f16[264,512]{1,0:T(8,128)(2,1)S(1)} %get-tuple-element.10), channel_id=1, source_target_pairs={{0,4},{4,8},{8,12},{12,0},{1,5},{5,9},{9,13},{13,1},{2,6},{6,10},{... | collective-permute-start | bytes 811016 | tf_op jit(solution)/shard_map/ppermute | solution.py:212
  17.6 2.4 %copy-start.1 = (bf16[768,1024]{1,0:T(8,128)(2,1)S(1)}, bf16[768,1024]{1,0:T(8,128)(2,1)}, u32[]{:S(2)}) copy-start(bf16[768,1024]{1,0:T(8,128)(2,1)} %own_ref.3) | copy-start | bytes 4718596
  17.9 15.3 %collective-permute-start.4 = (f16[264,1024]{1,0:T(8,128)(2,1)S(1)}, f16[264,1024]{1,0:T(8,128)(2,1)S(1)}, u32[]{:S(2)}, u32[]{:S(2)}) collective-permute-start(f16[264,1024]{1,0:T(8,128)(2,1)S(1)} %get-tuple-element.13), channel_id=1, source_target_pairs={{0,12},{4,0},{8,4},{12,8},{1,13},{5,1},{9,5},{13,9},{2,14},{6,2},{... | collective-permute-start | bytes 1622024 | tf_op jit(solution)/shard_map/ppermute | solution.py:212
  18.4 16.4 %collective-permute-start.2 = (f16[264,1024]{1,0:T(8,128)(2,1)S(1)}, f16[264,1024]{1,0:T(8,128)(2,1)S(1)}, u32[]{:S(2)}, u32[]{:S(2)}) collective-permute-start(f16[264,1024]{1,0:T(8,128)(2,1)S(1)} %get-tuple-element.14), channel_id=1, source_target_pairs={{0,4},{4,8},{8,12},{12,0},{1,5},{5,9},{9,13},{13,1},{2,6},{6,10},{... | collective-permute-start | bytes 1622024 | tf_op jit(solution)/shard_map/ppermute | solution.py:212
  22.7 18.9 %collective-permute-start.9 = (f16[520,512]{1,0:T(8,128)(2,1)S(1)}, f16[520,512]{1,0:T(8,128)(2,1)S(1)}, u32[]{:S(2)}, u32[]{:S(2)}) collective-permute-start(f16[520,512]{1,0:T(8,128)(2,1)S(1)} %slice_bitcast_fusion.2), channel_id=1, source_target_pairs={{0,128},{128,0},{1,129},{129,1},{2,130},{130,2},{3,131},{131,3},{4... | collective-permute-start | bytes 1597448 | tf_op jit(solution)/shard_map/ppermute | solution.py:212
  25.5 13.5 %collective-permute-start.6 = (f16[264,512]{1,0:T(8,128)(2,1)S(1)}, f16[264,512]{1,0:T(8,128)(2,1)S(1)}, u32[]{:S(2)}, u32[]{:S(2)}) collective-permute-start(f16[264,512]{1,0:T(8,128)(2,1)S(1)} %get-tuple-element.11), channel_id=1, source_target_pairs={{0,4},{4,8},{8,12},{12,0},{1,5},{5,9},{9,13},{13,1},{2,6},{6,10},{... | collective-permute-start | bytes 811016 | tf_op jit(solution)/shard_map/ppermute | solution.py:212
  25.6 13.5 %collective-permute-start.7 = (f16[264,512]{1,0:T(8,128)(2,1)S(1)}, f16[264,512]{1,0:T(8,128)(2,1)S(1)}, u32[]{:S(2)}, u32[]{:S(2)}) collective-permute-start(f16[264,512]{1,0:T(8,128)(2,1)S(1)} %get-tuple-element.12), channel_id=1, source_target_pairs={{0,12},{4,0},{8,4},{12,8},{1,13},{5,1},{9,5},{13,9},{2,14},{6,2},{... | collective-permute-start | bytes 811016 | tf_op jit(solution)/shard_map/ppermute | solution.py:212
  35.7 14.5 %collective-permute-start.5 = (f16[136,1024]{1,0:T(8,128)(2,1)S(1)}, f16[136,1024]{1,0:T(8,128)(2,1)S(1)}, u32[]{:S(2)}, u32[]{:S(2)}) collective-permute-start(f16[136,1024]{1,0:T(8,128)(2,1)S(1)} %fusion.1), channel_id=1, source_target_pairs={{0,128},{128,0},{1,129},{129,1},{2,130},{130,2},{3,131},{131,3},{4... | collective-permute-start | bytes 835592 | tf_op jit(solution)/shard_map/ppermute | solution.py:212
  39.5 6.5 %collective-permute-start.10 = (f16[264,256]{1,0:T(8,128)(2,1)S(1)}, f16[264,256]{1,0:T(8,128)(2,1)S(1)}, u32[]{:S(2)}, u32[]{:S(2)}) collective-permute-start(f16[264,256]{1,0:T(8,128)(2,1)S(1)} %get-tuple-element.20), channel_id=1, source_target_pairs={{0,12},{4,0},{8,4},{12,8},{1,13},{5,1},{9,5},{13,9},{2,14},{6,2},{... | collective-permute-start | bytes 405512 | tf_op jit(solution)/shard_map/ppermute | solution.py:212
  39.8 6.4 %collective-permute-start.8 = (f16[264,256]{1,0:T(8,128)(2,1)S(1)}, f16[264,256]{1,0:T(8,128)(2,1)S(1)}, u32[]{:S(2)}, u32[]{:S(2)}) collective-permute-start(f16[264,256]{1,0:T(8,128)(2,1)S(1)} %get-tuple-element.21), channel_id=1, source_target_pairs={{0,4},{4,8},{8,12},{12,0},{1,5},{5,9},{9,13},{13,1},{2,6},{6,10},{... | collective-permute-start | bytes 405512 | tf_op jit(solution)/shard_map/ppermute | solution.py:212
  42.3 8.0 %collective-permute-start.14 = (f16[136,512]{1,0:T(8,128)(2,1)S(1)}, f16[136,512]{1,0:T(8,128)(2,1)S(1)}, u32[]{:S(2)}, u32[]{:S(2)}) collective-permute-start(f16[136,512]{1,0:T(8,128)(2,1)S(1)} %get-tuple-element.15), channel_id=1, source_target_pairs={{0,12},{4,0},{8,4},{12,8},{1,13},{5,1},{9,5},{13,9},{2,14},{6,2},{... | collective-permute-start | bytes 417800 | tf_op jit(solution)/shard_map/ppermute | solution.py:212
  43.8 6.7 %collective-permute-start.13 = (f16[136,512]{1,0:T(8,128)(2,1)S(1)}, f16[136,512]{1,0:T(8,128)(2,1)S(1)}, u32[]{:S(2)}, u32[]{:S(2)}) collective-permute-start(f16[136,512]{1,0:T(8,128)(2,1)S(1)} %get-tuple-element.16), channel_id=1, source_target_pairs={{0,8},{4,12},{8,0},{12,4},{1,9},{5,13},{9,1},{13,5},{2,10},{6,14},... | collective-permute-start | bytes 417800 | tf_op jit(solution)/shard_map/ppermute | solution.py:212
  46.0 6.3 %collective-permute-start.12 = (f16[136,512]{1,0:T(8,128)(2,1)S(1)}, f16[136,512]{1,0:T(8,128)(2,1)S(1)}, u32[]{:S(2)}, u32[]{:S(2)}) collective-permute-start(f16[136,512]{1,0:T(8,128)(2,1)S(1)} %get-tuple-element.17), channel_id=1, source_target_pairs={{0,4},{4,8},{8,12},{12,0},{1,5},{5,9},{9,13},{13,1},{2,6},{6,10},{... | collective-permute-start | bytes 417800 | tf_op jit(solution)/shard_map/ppermute | solution.py:212
  46.6 6.7 %collective-permute-start.11 = (f16[136,512]{1,0:T(8,128)(2,1)S(1)}, f16[136,512]{1,0:T(8,128)(2,1)S(1)}, u32[]{:S(2)}, u32[]{:S(2)}) collective-permute-start(f16[136,512]{1,0:T(8,128)(2,1)S(1)} %fusion.2), channel_id=1, source_target_pairs={{0,128},{128,0},{1,129},{129,1},{2,130},{130,2},{3,131},{131,3},{4... | collective-permute-start | bytes 417800 | tf_op jit(solution)/shard_map/ppermute | solution.py:212

commit v6 on v5

--- a/solution.py
+++ b/solution.py
@@ -238,10 +238,12 @@
     got_left = passed(left_sent, "yh", 1)
     behind, beyond = long(passed(right_sent[0], "x", 1)), long(passed(right_sent[1], "x", NX - 1))
 
-    ahead_of = long(jnp.concatenate([right_sent[1], left_sent[: right_sent[1].shape[0]]], axis=1))
+    relay = call(join_kernel, "join", [(2, NY * NZ * rows + 8, quarter)], (right, 3), behind, beyond)
+    joined_sent = [short(relay[0]), short(relay[1])]
+    got_right = [passed(joined_sent[0], "x", 1), passed(joined_sent[1], "x", NX - 1)]
+
+    ahead_of = long(jnp.concatenate([*joined_sent, left_sent[: relay.shape[1]]], axis=1))
     got_first = [long(g) + 0.0 * ahead_of for g in got_first]
-    relay = call(join_kernel, "join", [(2, NY * NZ * rows + 8, quarter)], (right, 3), behind, beyond)
-    got_right = [passed(short(relay[0]), "x", 1), passed(short(relay[1]), "x", NX - 1)]
 
     lines = NZ * rows + 8
     over_two = functools.partial(x_to_y_kernel, (0, 1, NX - 1))

time: 78.4 us -> 82.4 us (1.051)
  waiting for transfers between devices: 20.9 us -> 25.8 us
  starting transfers between devices: 21.2 us -> 18.7 us
  blocking collectives: 23.2 us -> 24.3 us
    ppermute x15, waiting for transfers between devices: 20.9 us -> 25.8 us  [passed(): lax.ppermute(value, axis, [(i, (i + by) % count) for i in range(count)])]
    ppermute x15, starting transfers between devices: 21.2 us -> 18.7 us  [passed(): lax.ppermute(value, axis, [(i, (i + by) % count) for i in range(count)])]
    all_to_all x1, blocking collectives: 23.2 us -> 24.3 us  [per_device(): got = lax.all_to_all(short(sent), 'z', 0, 0, tiled=True)]
  transfers between devices with their start and end apart: 15 -> 15, of which waited for: 9 -> 8; matrix products, arithmetic and copies ran while one was open for 4% -> 4% of each run, Pallas kernels for 8% -> 8%
where the time goes in v6:
time: 82.4 us; the launch traced here: 81.3 us
  waiting for transfers between devices  25.8 us (31%)
  blocking collectives  24.3 us (29%)
  starting transfers between devices  18.7 us (23%)
  Pallas kernels  7.66 us (9%)
  other arithmetic  2.36 us (3%)
  local copies, waits for them, and re-layouts  2.2 us (3%)
    ppermute x15, waiting for transfers between devices, passed(): lax.ppermute(value, axis, [(i, (i + by) % count) for i in range(count)])  25.8 us
    all_to_all x1, blocking collectives, per_device(): got = lax.all_to_all(short(sent), 'z', 0, 0, tiled=True)  24.3 us
    ppermute x15, starting transfers between devices, passed(): lax.ppermute(value, axis, [(i, (i + by) % count) for i in range(count)])  18.7 us
    pallas_call x9, Pallas kernels, call(): pl.pallas_call(kernel, grid=(1,), out_shape=out_shape, in_specs=specs, ou...  7.66 us
  transfers between devices with their start and end apart: 15, of which 8 were waited for; matrix products, arithmetic and copies ran while one was open for 4% of the time, Pallas kernels for 8%

profile of v6, /device:TPU:8, one launch (start us, length us, event | category | flops | bytes accessed | tf_op | source)
XLA Modules:
  0.0 81.3 jit_solution(1940940685908415410)
XLA Ops:
  0.0 1.4 %copy-done = bf16[768,1024]{1,0:T(8,128)(2,1)S(1)} copy-done((bf16[768,1024]{1,0:T(8,128)(2,1)S(1)}, bf16[768,1024]{1,0:T(8,128)(2,1)}, u32[]{:S(2)}) %copy-start) | copy-done | bytes 1572888
  1.4 2.3 %diagonal.1.next_ref.before_ref.own_ref = f32[4,264,1024]{2,1,0:T(8,128)S(1)} custom-call(bf16[768,1024]{1,0:T(8,128)(2,1)S(1)} %copy-done, bf16[768,1024]{1,0:T(8,128)(2,1)S(1)} %copy-done), custom_call_target="tpu_custom_call" | custom-call | flops 1610612736 | bytes 7471104 | tf_op jit(solution)/shard_map/diagonal/pallas_call | solution.py:197
  3.7 0.4 convert.30
  4.3 2.8 %collective-permute-start.1 = (f16[264,512]{1,0:T(8,128)(2,1)S(1)}, f16[264,512]{1,0:T(8,128)(2,1)S(1)}, u32[]{:S(2)}, u32[]{:S(2)}) collective-permute-start(f16[264,512]{1,0:T(8,128)(2,1)S(1)} %get-tuple-element.9), channel_id=1, source_target_pairs={{0,12},{4,0},{8,4},{12,8},{1,13},{5,1},{9,5},{13,9},{2,14},{6,2},{... | collective-permute-start | bytes 811016 | tf_op jit(solution)/shard_map/ppermute | solution.py:212
  7.1 6.4 %collective-permute-done.1 = f16[264,512]{1,0:T(8,128)(2,1)S(1)} collective-permute-done((f16[264,512]{1,0:T(8,128)(2,1)S(1)}, f16[264,512]{1,0:T(8,128)(2,1)S(1)}, u32[]{:S(2)}, u32[]{:S(2)}) %collective-permute-start.1) | collective-permute-done | bytes 270368 | tf_op jit(solution)/shard_map/ppermute | solution.py:212
  13.6 3.3 %collective-permute-done = f16[264,512]{1,0:T(8,128)(2,1)S(1)} collective-permute-done((f16[264,512]{1,0:T(8,128)(2,1)S(1)}, f16[264,512]{1,0:T(8,128)(2,1)S(1)}, u32[]{:S(2)}, u32[]{:S(2)}) %collective-permute-start) | collective-permute-done | bytes 270368 | tf_op jit(solution)/shard_map/ppermute | solution.py:212
  17.0 0.4 relay.1._
  17.7 0.3 slice_bitcast_fusion
  17.9 0.4 collective-permute-start.6
  18.4 1.7 %collective-permute-start.2 = (f16[264,1024]{1,0:T(8,128)(2,1)S(1)}, f16[264,1024]{1,0:T(8,128)(2,1)S(1)}, u32[]{:S(2)}, u32[]{:S(2)}) collective-permute-start(f16[264,1024]{1,0:T(8,128)(2,1)S(1)} %get-tuple-element.12), channel_id=1, source_target_pairs={{0,4},{4,8},{8,12},{12,0},{1,5},{5,9},{9,13},{13,1},{2,6},{6,10},{... | collective-permute-start | bytes 1622024 | tf_op jit(solution)/shard_map/ppermute | solution.py:212
  20.1 2.3 %beside.1 = (f32[2,520,512]{2,1,0:T(8,128)S(1)}, f32[4,264,512]{2,1,0:T(8,128)S(1)}) custom-call(bf16[768,1024]{1,0:T(8,128)(2,1)S(1)} %copy-done.1, bf16[768,1024]{1,0:T(8,128)(2,1)S(1)} %collective-permute-done.3.partner_ref, f32[2,264,1024]{2,1,0:T(8,128)S(1)} %relay.1._), custom_call_target="tpu_custom_call" | custom-call | flops 1610612736 | bytes 9601024 | tf_op jit(solution)/shard_map/beside/pallas_call | solution.py:197
  23.0 1.6 %collective-permute-start.5 = (f16[264,512]{1,0:T(8,128)(2,1)S(1)}, f16[264,512]{1,0:T(8,128)(2,1)S(1)}, u32[]{:S(2)}, u32[]{:S(2)}) collective-permute-start(f16[264,512]{1,0:T(8,128)(2,1)S(1)} %get-tuple-element.13), channel_id=1, source_target_pairs={{0,12},{4,0},{8,4},{12,8},{1,13},{5,1},{9,5},{13,9},{2,14},{6,2},{... | collective-permute-start | bytes 811016 | tf_op jit(solution)/shard_map/ppermute | solution.py:212
  24.7 0.5 collective-permute-start.4
  25.2 2.5 %collective-permute-start.9 = (f16[520,512]{1,0:T(8,128)(2,1)S(1)}, f16[520,512]{1,0:T(8,128)(2,1)S(1)}, u32[]{:S(2)}, u32[]{:S(2)}) collective-permute-start(f16[520,512]{1,0:T(8,128)(2,1)S(1)} %slice_bitcast_fusion.2), channel_id=1, source_target_pairs={{0,128},{128,0},{1,129},{129,1},{2,130},{130,2},{3,131},{131,3},{4... | collective-permute-start | bytes 1597448 | tf_op jit(solution)/shard_map/ppermute | solution.py:212
  27.8 9.6 %collective-permute-done.5 = f16[264,512]{1,0:T(8,128)(2,1)S(1)} collective-permute-done((f16[264,512]{1,0:T(8,128)(2,1)S(1)}, f16[264,512]{1,0:T(8,128)(2,1)S(1)}, u32[]{:S(2)}, u32[]{:S(2)}) %collective-permute-start.5) | collective-permute-done | bytes 270368 | tf_op jit(solution)/shard_map/ppermute | solution.py:212
  37.4 1.5 %collective-permute-done.4 = f16[264,512]{1,0:T(8,128)(2,1)S(1)} collective-permute-done((f16[264,512]{1,0:T(8,128)(2,1)S(1)}, f16[264,512]{1,0:T(8,128)(2,1)S(1)}, u32[]{:S(2)}, u32[]{:S(2)}) %collective-permute-start.4) | collective-permute-done | bytes 270368 | tf_op jit(solution)/shard_map/ppermute | solution.py:212
  39.1 0.3 join.1
  39.6 3.1 %collective-permute-start.10 = (f16[264,256]{1,0:T(8,128)(2,1)S(1)}, f16[264,256]{1,0:T(8,128)(2,1)S(1)}, u32[]{:S(2)}, u32[]{:S(2)}) collective-permute-start(f16[264,256]{1,0:T(8,128)(2,1)S(1)} %get-tuple-element.21), channel_id=1, source_target_pairs={{0,12},{4,0},{8,4},{12,8},{1,13},{5,1},{9,5},{13,9},{2,14},{6,2},{... | collective-permute-start | bytes 405512 | tf_op jit(solution)/shard_map/ppermute | solution.py:212
  42.8 0.3 convert_add_fusion
  43.1 0.5 first_x.1.refs_0_
  43.7 2.1 %collective-permute-start.7 = (f16[136,1024]{1,0:T(8,128)(2,1)S(1)}, f16[136,1024]{1,0:T(8,128)(2,1)S(1)}, u32[]{:S(2)}, u32[]{:S(2)}) collective-permute-start(f16[136,1024]{1,0:T(8,128)(2,1)S(1)} %fusion.1), channel_id=1, source_target_pairs={{0,128},{128,0},{1,129},{129,1},{2,130},{130,2},{3,131},{131,3},{4... | collective-permute-start | bytes 835592 | tf_op jit(solution)/shard_map/ppermute | solution.py:212
  45.9 0.4 left_y.1.refs_4_
  46.6 1.0 %collective-permute-start.13 = (f16[136,512]{1,0:T(8,128)(2,1)S(1)}, f16[136,512]{1,0:T(8,128)(2,1)S(1)}, u32[]{:S(2)}, u32[]{:S(2)}) collective-permute-start(f16[136,512]{1,0:T(8,128)(2,1)S(1)} %get-tuple-element.16), channel_id=1, source_target_pairs={{0,8},{4,12},{8,0},{12,4},{1,9},{5,13},{9,1},{13,5},{2,10},{6,14},... | collective-permute-start | bytes 417800 | tf_op jit(solution)/shard_map/ppermute | solution.py:212
  47.6 1.0 %collective-permute-start.12 = (f16[136,512]{1,0:T(8,128)(2,1)S(1)}, f16[136,512]{1,0:T(8,128)(2,1)S(1)}, u32[]{:S(2)}, u32[]{:S(2)}) collective-permute-start(f16[136,512]{1,0:T(8,128)(2,1)S(1)} %get-tuple-element.17), channel_id=1, source_target_pairs={{0,4},{4,8},{8,12},{12,0},{1,5},{5,9},{9,13},{13,1},{2,6},{6,10},{... | collective-permute-start | bytes 417800 | tf_op jit(solution)/shard_map/ppermute | solution.py:212
  48.7 0.3 right_x.1.refs_2_
  49.1 1.6 %collective-permute-start.11 = (f16[136,512]{1,0:T(8,128)(2,1)S(1)}, f16[136,512]{1,0:T(8,128)(2,1)S(1)}, u32[]{:S(2)}, u32[]{:S(2)}) collective-permute-start(f16[136,512]{1,0:T(8,128)(2,1)S(1)} %fusion.2), channel_id=1, source_target_pairs={{0,128},{128,0},{1,129},{129,1},{2,130},{130,2},{3,131},{131,3},{4... | collective-permute-start | bytes 417800 | tf_op jit(solution)/shard_map/ppermute | solution.py:212
  50.6 2.7 %collective-permute-done.7 = f16[136,1024]{1,0:T(8,128)(2,1)S(1)} collective-permute-done((f16[136,1024]{1,0:T(8,128)(2,1)S(1)}, f16[136,1024]{1,0:T(8,128)(2,1)S(1)}, u32[]{:S(2)}, u32[]{:S(2)}) %collective-permute-start.7) | collective-permute-done | bytes 278560 | tf_op jit(solution)/shard_map/ppermute | solution.py:212
  53.7 1.4 %collective-permute-done.12 = f16[136,512]{1,0:T(8,128)(2,1)S(1)} collective-permute-done((f16[136,512]{1,0:T(8,128)(2,1)S(1)}, f16[136,512]{1,0:T(8,128)(2,1)S(1)}, u32[]{:S(2)}, u32[]{:S(2)}) %collective-permute-start.12) | collective-permute-done | bytes 139296 | tf_op jit(solution)/shard_map/ppermute | solution.py:212
  55.1 0.6 collective-permute-done.11
  55.7 0.4 to_z.1
  56.2 24.3 %all_to_all.5 = f16[8,16,2176]{2,1,0:T(8,128)(2,1)S(1)} all-to-all(f16[8,16,2176]{2,1,0:T(8,128)(2,1)S(1)} %convert_element_type.144), channel_id=1, replica_groups=mesh['yh'=2,'z'=8,'x'=4,'yl'=2,'core'=2] {'z'}, dimensions={0} | all-to-all | bytes 1114112 | tf_op jit(solution)/shard_map/all_to_all | solution.py:264
  80.6 0.7 z_sum.1
  (42 shorter events, 2.6 us)
Async XLA Ops:
  0.0 20.1 %collective-permute-start.3 = (bf16[768,1024]{1,0:T(8,128)(2,1)}, bf16[768,1024]{1,0:T(8,128)(2,1)S(1)}, u32[]{:S(2)}, u32[]{:S(2)}) collective-permute-start(bf16[768,1024]{1,0:T(8,128)(2,1)} %own_ref.3), channel_id=1, source_target_pairs={{0,3},{1,0},{2,1},{3,2},{4,7},{5,4},{6,5},{7,6},{8,11},{9,8},{10,9... | collective-permute-start | bytes 4718600 | tf_op jit(solution)/shard_map/ppermute | solution.py:212
  0.0 1.4 %copy-start = (bf16[768,1024]{1,0:T(8,128)(2,1)S(1)}, bf16[768,1024]{1,0:T(8,128)(2,1)}, u32[]{:S(2)}) copy-start(bf16[768,1024]{1,0:T(8,128)(2,1)} %own_ref.3) | copy-start | bytes 4718596
  4.3 9.2 %collective-permute-start.1 = (f16[264,512]{1,0:T(8,128)(2,1)S(1)}, f16[264,512]{1,0:T(8,128)(2,1)S(1)}, u32[]{:S(2)}, u32[]{:S(2)}) collective-permute-start(f16[264,512]{1,0:T(8,128)(2,1)S(1)} %get-tuple-element.9), channel_id=1, source_target_pairs={{0,12},{4,0},{8,4},{12,8},{1,13},{5,1},{9,5},{13,9},{2,14},{6,2},{... | collective-permute-start | bytes 811016 | tf_op jit(solution)/shard_map/ppermute | solution.py:212
  7.1 9.8 %collective-permute-start = (f16[264,512]{1,0:T(8,128)(2,1)S(1)}, f16[264,512]{1,0:T(8,128)(2,1)S(1)}, u32[]{:S(2)}, u32[]{:S(2)}) collective-permute-start(f16[264,512]{1,0:T(8,128)(2,1)S(1)} %get-tuple-element.10), channel_id=1, source_target_pairs={{0,4},{4,8},{8,12},{12,0},{1,5},{5,9},{9,13},{13,1},{2,6},{6,10},{... | collective-permute-start | bytes 811016 | tf_op jit(solution)/shard_map/ppermute | solution.py:212
  17.7 2.4 %copy-start.1 = (bf16[768,1024]{1,0:T(8,128)(2,1)S(1)}, bf16[768,1024]{1,0:T(8,128)(2,1)}, u32[]{:S(2)}) copy-start(bf16[768,1024]{1,0:T(8,128)(2,1)} %own_ref.3) | copy-start | bytes 4718596
  17.9 24.8 %collective-permute-start.6 = (f16[264,1024]{1,0:T(8,128)(2,1)S(1)}, f16[264,1024]{1,0:T(8,128)(2,1)S(1)}, u32[]{:S(2)}, u32[]{:S(2)}) collective-permute-start(f16[264,1024]{1,0:T(8,128)(2,1)S(1)} %get-tuple-element.11), channel_id=1, source_target_pairs={{0,12},{4,0},{8,4},{12,8},{1,13},{5,1},{9,5},{13,9},{2,14},{6,2},{... | collective-permute-start | bytes 1622024 | tf_op jit(solution)/shard_map/ppermute | solution.py:212
  18.4 24.4 %collective-permute-start.2 = (f16[264,1024]{1,0:T(8,128)(2,1)S(1)}, f16[264,1024]{1,0:T(8,128)(2,1)S(1)}, u32[]{:S(2)}, u32[]{:S(2)}) collective-permute-start(f16[264,1024]{1,0:T(8,128)(2,1)S(1)} %get-tuple-element.12), channel_id=1, source_target_pairs={{0,4},{4,8},{8,12},{12,0},{1,5},{5,9},{9,13},{13,1},{2,6},{6,10},{... | collective-permute-start | bytes 1622024 | tf_op jit(solution)/shard_map/ppermute | solution.py:212
  23.0 14.4 %collective-permute-start.5 = (f16[264,512]{1,0:T(8,128)(2,1)S(1)}, f16[264,512]{1,0:T(8,128)(2,1)S(1)}, u32[]{:S(2)}, u32[]{:S(2)}) collective-permute-start(f16[264,512]{1,0:T(8,128)(2,1)S(1)} %get-tuple-element.13), channel_id=1, source_target_pairs={{0,12},{4,0},{8,4},{12,8},{1,13},{5,1},{9,5},{13,9},{2,14},{6,2},{... | collective-permute-start | bytes 811016 | tf_op jit(solution)/shard_map/ppermute | solution.py:212
  24.7 14.3 %collective-permute-start.4 = (f16[264,512]{1,0:T(8,128)(2,1)S(1)}, f16[264,512]{1,0:T(8,128)(2,1)S(1)}, u32[]{:S(2)}, u32[]{:S(2)}) collective-permute-start(f16[264,512]{1,0:T(8,128)(2,1)S(1)} %get-tuple-element.14), channel_id=1, source_target_pairs={{0,4},{4,8},{8,12},{12,0},{1,5},{5,9},{9,13},{13,1},{2,6},{6,10},{... | collective-permute-start | bytes 811016 | tf_op jit(solution)/shard_map/ppermute | solution.py:212
  25.2 20.6 %collective-permute-start.9 = (f16[520,512]{1,0:T(8,128)(2,1)S(1)}, f16[520,512]{1,0:T(8,128)(2,1)S(1)}, u32[]{:S(2)}, u32[]{:S(2)}) collective-permute-start(f16[520,512]{1,0:T(8,128)(2,1)S(1)} %slice_bitcast_fusion.2), channel_id=1, source_target_pairs={{0,128},{128,0},{1,129},{129,1},{2,130},{130,2},{3,131},{131,3},{4... | collective-permute-start | bytes 1597448 | tf_op jit(solution)/shard_map/ppermute | solution.py:212
  39.4 8.1 %collective-permute-start.8 = (f16[264,256]{1,0:T(8,128)(2,1)S(1)}, f16[264,256]{1,0:T(8,128)(2,1)S(1)}, u32[]{:S(2)}, u32[]{:S(2)}) collective-permute-start(f16[264,256]{1,0:T(8,128)(2,1)S(1)} %get-tuple-element.20), channel_id=1, source_target_pairs={{0,4},{4,8},{8,12},{12,0},{1,5},{5,9},{9,13},{13,1},{2,6},{6,10},{... | collective-permute-start | bytes 405512 | tf_op jit(solution)/shard_map/ppermute | solution.py:212
  39.6 9.0 %collective-permute-start.10 = (f16[264,256]{1,0:T(8,128)(2,1)S(1)}, f16[264,256]{1,0:T(8,128)(2,1)S(1)}, u32[]{:S(2)}, u32[]{:S(2)}) collective-permute-start(f16[264,256]{1,0:T(8,128)(2,1)S(1)} %get-tuple-element.21), channel_id=1, source_target_pairs={{0,12},{4,0},{8,4},{12,8},{1,13},{5,1},{9,5},{13,9},{2,14},{6,2},{... | collective-permute-start | bytes 405512 | tf_op jit(solution)/shard_map/ppermute | solution.py:212
  43.7 9.6 %collective-permute-start.7 = (f16[136,1024]{1,0:T(8,128)(2,1)S(1)}, f16[136,1024]{1,0:T(8,128)(2,1)S(1)}, u32[]{:S(2)}, u32[]{:S(2)}) collective-permute-start(f16[136,1024]{1,0:T(8,128)(2,1)S(1)} %fusion.1), channel_id=1, source_target_pairs={{0,128},{128,0},{1,129},{129,1},{2,130},{130,2},{3,131},{131,3},{4... | collective-permute-start | bytes 835592 | tf_op jit(solution)/shard_map/ppermute | solution.py:212
  46.5 6.9 %collective-permute-start.14 = (f16[136,512]{1,0:T(8,128)(2,1)S(1)}, f16[136,512]{1,0:T(8,128)(2,1)S(1)}, u32[]{:S(2)}, u32[]{:S(2)}) collective-permute-start(f16[136,512]{1,0:T(8,128)(2,1)S(1)} %get-tuple-element.15), channel_id=1, source_target_pairs={{0,12},{4,0},{8,4},{12,8},{1,13},{5,1},{9,5},{13,9},{2,14},{6,2},{... | collective-permute-start | bytes 417800 | tf_op jit(solution)/shard_map/ppermute | solution.py:212
  46.6 7.0 %collective-permute-start.13 = (f16[136,512]{1,0:T(8,128)(2,1)S(1)}, f16[136,512]{1,0:T(8,128)(2,1)S(1)}, u32[]{:S(2)}, u32[]{:S(2)}) collective-permute-start(f16[136,512]{1,0:T(8,128)(2,1)S(1)} %get-tuple-element.16), channel_id=1, source_target_pairs={{0,8},{4,12},{8,0},{12,4},{1,9},{5,13},{9,1},{13,5},{2,10},{6,14},... | collective-permute-start | bytes 417800 | tf_op jit(solution)/shard_map/ppermute | solution.py:212
  47.6 7.5 %collective-permute-start.12 = (f16[136,512]{1,0:T(8,128)(2,1)S(1)}, f16[136,512]{1,0:T(8,128)(2,1)S(1)}, u32[]{:S(2)}, u32[]{:S(2)}) collective-permute-start(f16[136,512]{1,0:T(8,128)(2,1)S(1)} %get-tuple-element.17), channel_id=1, source_target_pairs={{0,4},{4,8},{8,12},{12,0},{1,5},{5,9},{9,13},{13,1},{2,6},{6,10},{... | collective-permute-start | bytes 417800 | tf_op jit(solution)/shard_map/ppermute | solution.py:212
  49.1 6.6 %collective-permute-start.11 = (f16[136,512]{1,0:T(8,128)(2,1)S(1)}, f16[136,512]{1,0:T(8,128)(2,1)S(1)}, u32[]{:S(2)}, u32[]{:S(2)}) collective-permute-start(f16[136,512]{1,0:T(8,128)(2,1)S(1)} %fusion.2), channel_id=1, source_target_pairs={{0,128},{128,0},{1,129},{129,1},{2,130},{130,2},{3,131},{131,3},{4... | collective-permute-start | bytes 417800 | tf_op jit(solution)/shard_map/ppermute | solution.py:212
